TPU v7x, 32 devices: a whole 2x2x4 slice. The times are simulated.
32 devices in a mesh: frame: 4 (over z), panel: 8 (over y, x, core).
Axes of the slice: x: 2, y: 2, z: 4, core: 2. Of those that a mesh axis runs over, the one named last changes fastest.
Arguments:
- spline_index: int32 [4096, 2, 4, 256], P(('frame', 'panel')), may hold values from 0 to 124
- spline_frac: bfloat16 [4096, 2, 4, 256], P(('frame', 'panel')), may hold values from 0 to 1
- projection: bfloat16 [4096, 2, 4, 256], P(('frame', 'panel')), may hold values from -6 to 6
- forces: bfloat16 [4096, 256], P(('frame', 'panel')), may hold values from -6 to 6
- row_owner: int32 [4096, 1], P(('frame', 'panel')), may hold values from 0 to 31, as said below
- row_offset: int32 [4096], P(('frame', 'panel')), may hold values from 0 to 21
Outputs:
- normal_band: float32 [704, 2, 128, 128], P(('frame', 'panel'))
- normal_rhs: float32 [704, 128], P(('frame', 'panel'))
Inputs may be any that keep to these rules, and one draw needn't show every extreme that they name: `row_owner`: among the row tiles of one device, no owner index is named by more than 8 tiles, and some owner index is named by exactly 8. Every owner index is named by some row tile.
All inputs are finite; a program needn't handle non-finite values.
Results may differ from a plain program's by a relative error of at most 0.0029.
Values may be sent and summed in bfloat16 or wider, within the bound.
A program may use at most 64 MiB of HBM per device.

v0:
```python
import jax
import jax.numpy as jnp
from jax import lax
from jax.sharding import PartitionSpec as P

CO = 128
BLK_DEV = 22


def shifted(block, axis, distance):
    devices = range(lax.axis_size(axis))
    route = [((i - distance) % len(devices), i) for i in devices]
    return lax.ppermute(block, axis, route)


def basis_tiles(spline_index, spline_frac, projection, column_count):
    columns = lax.broadcasted_iota(jnp.int32, (1, 1, 1, column_count), 3)
    summed = jnp.zeros(spline_index.shape[:2] + (spline_index.shape[3], column_count), jnp.float32)
    for neighbor in range(spline_index.shape[2]):
        offset = columns - spline_index[:, :, neighbor, :, None]
        position = spline_frac[:, :, neighbor, :, None].astype(jnp.float32)
        weight = projection[:, :, neighbor, :, None].astype(jnp.float32)
        one_minus = 1.0 - position
        pos_square = position * position
        pos_cube = pos_square * position
        basis_zero = one_minus * one_minus * one_minus / 6.0
        basis_one = (3.0 * pos_cube - 6.0 * pos_square + 4.0) / 6.0
        basis_two = (-3.0 * pos_cube + 3.0 * pos_square + 3.0 * position + 1.0) / 6.0
        basis_three = pos_cube / 6.0
        basis_value = jnp.where(
            offset == 0,
            basis_zero,
            jnp.where(
                offset == 1,
                basis_one,
                jnp.where(offset == 2, basis_two, jnp.where(offset == 3, basis_three, 0.0)),
            ),
        )
        summed = summed + weight * basis_value
    return summed.astype(jnp.bfloat16)


def on_device(spline_index, spline_frac, projection, forces, row_owner, row_offset):
    row_count = spline_index.shape[0]
    slot_width = spline_index.shape[1]
    device_count = lax.axis_size(("frame", "panel"))
    capacity = max(2, 2 * row_count // device_count)
    slot_count = device_count * capacity
    owners = row_owner[:, 0]
    same_owner = owners[:, None] == owners[None, :]
    order_index = lax.broadcasted_iota(jnp.int32, (row_count, row_count), 0)
    other_index = lax.broadcasted_iota(jnp.int32, (row_count, row_count), 1)
    position = jnp.sum((same_owner & (other_index < order_index)).astype(jnp.int32), axis=1)
    target = owners * capacity + position

    def place(values):
        empty = jnp.zeros((slot_count,) + values.shape[1:], values.dtype)
        return empty.at[target].set(values)

    send_index = place(spline_index)
    send_frac = place(spline_frac)
    send_proj = place(projection)
    send_force = place(forces)
    send_offset = place(row_offset)
    incoming = (
        lax.all_to_all(send_index, ("frame", "panel"), split_axis=0, concat_axis=0, tiled=True),
        lax.all_to_all(send_frac, ("frame", "panel"), split_axis=0, concat_axis=0, tiled=True),
        lax.all_to_all(send_proj, ("frame", "panel"), split_axis=0, concat_axis=0, tiled=True),
        lax.all_to_all(send_force, ("frame", "panel"), split_axis=0, concat_axis=0, tiled=True),
        lax.all_to_all(send_offset, ("frame", "panel"), split_axis=0, concat_axis=0, tiled=True),
    )
    batch_size = 16
    turns = slot_count // batch_size

    def split(member):
        return member.reshape((turns, batch_size) + member.shape[1:])

    def accumulate(totals, pieces):
        band_acc, rhs_acc = totals
        index_part, frac_part, proj_part, force_part, offset_part = pieces
        design = basis_tiles(index_part, frac_part, proj_part, CO)
        for band_lag in range(slot_width):
            left_tiles = design[:, : slot_width - band_lag]
            right_tiles = design[:, band_lag:]
            products = jnp.einsum(
                "bsxi,bsxj->bsij", left_tiles, right_tiles, preferred_element_type=jnp.float32
            )
            rows_at = offset_part[:, None] + lax.broadcasted_iota(
                jnp.int32, (1, slot_width - band_lag), 1
            )
            band_acc = band_acc.at[rows_at, band_lag].add(products)
        moments = jnp.einsum("bsxi,bx->bsi", design, force_part, preferred_element_type=jnp.float32)
        rows_all = offset_part[:, None] + lax.broadcasted_iota(jnp.int32, (1, slot_width), 1)
        rhs_acc = rhs_acc.at[rows_all].add(moments)
        return ((band_acc, rhs_acc), None)

    acc_rows = BLK_DEV + slot_width - 1
    band_init = jnp.zeros((acc_rows, slot_width, CO, CO), jnp.float32)
    rhs_init = jnp.zeros((acc_rows, CO), jnp.float32)
    (band_acc, rhs_acc), unused = lax.scan(
        accumulate,
        (band_init, rhs_init),
        (
            split(incoming[0]),
            split(incoming[1]),
            split(incoming[2]),
            split(incoming[3]),
            split(incoming[4]),
        ),
    )
    spill_band, spill_rhs = shifted((band_acc[BLK_DEV:], rhs_acc[BLK_DEV:]), ("frame", "panel"), 1)
    normal_band = band_acc[:BLK_DEV].at[: slot_width - 1].add(spill_band)
    normal_rhs = rhs_acc[:BLK_DEV].at[: slot_width - 1].add(spill_rhs)
    return (normal_band, normal_rhs)


def solution(mesh):
    in_specs = (
        P(("frame", "panel"), None, None, None),
        P(("frame", "panel"), None, None, None),
        P(("frame", "panel"), None, None, None),
        P(("frame", "panel"), None),
        P(("frame", "panel"), None),
        P(("frame", "panel")),
    )
    out_specs = (P(("frame", "panel"), None, None, None), P(("frame", "panel"), None))
    return jax.shard_map(
        on_device, mesh=mesh, in_specs=in_specs, out_specs=out_specs, check_vma=False
    )
```

profile of v0, /device:TPU:0, one launch (start us, length us, event | category | flops | bytes accessed | tf_op | source)
XLA Modules:
  0.0 877.3 jit_solution(15578883237610579937)
XLA Ops:
  4.0 7.3 all-to-all-start
  13.3 5.1 all-to-all-done
  22.3 16.5 %scatter_fusion.3 = bf16[256,2,4,256]{3,2,1,0:T(4,128)(2,1)} fusion(bf16[256,2,4,256]{3,2,1,0:T(4,128)(2,1)} %broadcast.416.clone, s32[128]{0:T(128)S(1)} %fusion.85, bf16[128,2,4,256]{3,2,1,0:T(4,128)(2,1)} %param.14), kind=kCustom, calls=%fused_computation.4 | custom fusion | bytes 1573376 | tf_op jit(solution)/shard_map/scatter | solution.py:58
  38.8 6.0 all-to-all-start.1
  46.1 14.4 %scatter_fusion.5 = bf16[256,2,4,256]{3,2,1,0:T(4,128)(2,1)} fusion(bf16[256,2,4,256]{3,2,1,0:T(4,128)(2,1)} %broadcast.416.clone.1, s32[128]{0:T(128)S(1)} %fusion.85, bf16[128,2,4,256]{3,2,1,0:T(4,128)(2,1)S(1)} %copy-done.5), kind=kCustom, calls=%fused_computation.6 | custom fusion | bytes 1573376 | tf_op jit(solution)/shard_map/scatter | solution.py:58
  60.5 10.5 %all-to-all-done.1 = bf16[256,2,4,256]{3,2,1,0:T(4,128)(2,1)} async-done(((bf16[256,2,4,256]{3,2,1,0:T(4,128)(2,1)}), bf16[256,2,4,256]{3,2,1,0:T(4,128)(2,1)}, u32[]{:S(2)}, u32[]{:S(2)}) %all-to-all-start.1) | async-done | bytes 1048608 | tf_op jit(solution)/shard_map/all_to_all | solution.py:68
  71.0 3.7 all-to-all-start.3
  76.4 13.7 %scatter_fusion.4 = s32[256,2,4,256]{3,2,1,0:T(4,128)} fusion(s32[256,2,4,256]{3,2,1,0:T(4,128)} %broadcast_in_dim.124, s32[128]{0:T(128)S(1)} %fusion.85, s32[128,2,4,256]{3,2,1,0:T(4,128)S(1)} %copy-done.4), kind=kCustom, calls=%fused_computation.5 | custom fusion | bytes 3146240 | tf_op jit(solution)/shard_map/scatter | solution.py:58
  90.0 11.0 %all-to-all-done.3 = bf16[256,2,4,256]{3,2,1,0:T(4,128)(2,1)} async-done(((bf16[256,2,4,256]{3,2,1,0:T(4,128)(2,1)}), bf16[256,2,4,256]{3,2,1,0:T(4,128)(2,1)}, u32[]{:S(2)}, u32[]{:S(2)}) %all-to-all-start.3) | async-done | bytes 1048608 | tf_op jit(solution)/shard_map/all_to_all | solution.py:67
  101.0 3.6 all-to-all-start.2
  106.0 47.5 %all-to-all-done.2 = s32[256,2,4,256]{3,2,1,0:T(4,128)S(1)} async-done(((s32[256,2,4,256]{3,2,1,0:T(4,128)}), s32[256,2,4,256]{3,2,1,0:T(4,128)S(1)}, u32[]{:S(2)}, u32[]{:S(2)}) %all-to-all-start.2) | async-done | bytes 2097184 | tf_op jit(solution)/shard_map/all_to_all | solution.py:66
  155.5 708.3 %while.14 = (s32[]{:T(128)}, f32[23,2,128,128]{3,2,1,0:T(8,128)}, f32[23,128]{1,0:T(8,128)S(1)}, s32[16,16]{1,0:T(8,128)S(1)}, bf16[16,16,2,4,256]{4,3,2,1,0:T(4...) while((s32[]{:T(128)}, f32[23,2,128,128]{3,2,1,0:T(8,128)}, ...), condition=%wide.region_10.11_spmd, body=%wide.region_6.10_spmd.sunk | while | flops 452366784 | bytes 40724592 | solution.py:100
  157.2 27.9 %add_convert_fusion.2 = bf16[16,2,256,128]{3,2,0,1:T(8,128)(2,1)S(1)} fusion(f32[16,2,256]{2,0,1:T(8,128)S(1)} %get-tuple-element.218, f32[16,2,256]{2,0,1:T(8,128)S(1)} %get-tuple-element.219, f32[16,2,256]{2,0,1:T(8,128)S(1)} %get-tuple-element.220, f32[16,2,256]{2,0,1:T(8,128)S(1)} %get-tuple-element.221, s32[16,2,256]{2,0,1:T(8,128)S(1)} %get-tuple-element.222, ...), kind=kLoop, calls=%fused_computation.8.clone.1 | loop fusion | flops 46137344 | bytes 2883584 | tf_op jit(solution)/shard_map/while/body/eval_jaxpr/convert_element_type | solution.py:40
  188.8 7.4 scatter_fusion
  201.4 27.9 %add_convert_fusion.2 = bf16[16,2,256,128]{3,2,0,1:T(8,128)(2,1)S(1)} fusion(f32[16,2,256]{2,0,1:T(8,128)S(1)} %get-tuple-element.218, f32[16,2,256]{2,0,1:T(8,128)S(1)} %get-tuple-element.219, f32[16,2,256]{2,0,1:T(8,128)S(1)} %get-tuple-element.220, f32[16,2,256]{2,0,1:T(8,128)S(1)} %get-tuple-element.221, s32[16,2,256]{2,0,1:T(8,128)S(1)} %get-tuple-element.222, ...), kind=kLoop, calls=%fused_computation.8.clone.1 | loop fusion | flops 46137344 | bytes 2883584 | tf_op jit(solution)/shard_map/while/body/eval_jaxpr/convert_element_type | solution.py:40
  233.0 7.2 scatter_fusion
  245.3 27.9 %add_convert_fusion.2 = bf16[16,2,256,128]{3,2,0,1:T(8,128)(2,1)S(1)} fusion(f32[16,2,256]{2,0,1:T(8,128)S(1)} %get-tuple-element.218, f32[16,2,256]{2,0,1:T(8,128)S(1)} %get-tuple-element.219, f32[16,2,256]{2,0,1:T(8,128)S(1)} %get-tuple-element.220, f32[16,2,256]{2,0,1:T(8,128)S(1)} %get-tuple-element.221, s32[16,2,256]{2,0,1:T(8,128)S(1)} %get-tuple-element.222, ...), kind=kLoop, calls=%fused_computation.8.clone.1 | loop fusion | flops 46137344 | bytes 2883584 | tf_op jit(solution)/shard_map/while/body/eval_jaxpr/convert_element_type | solution.py:40
  276.9 7.4 scatter_fusion
  289.5 27.9 %add_convert_fusion.2 = bf16[16,2,256,128]{3,2,0,1:T(8,128)(2,1)S(1)} fusion(f32[16,2,256]{2,0,1:T(8,128)S(1)} %get-tuple-element.218, f32[16,2,256]{2,0,1:T(8,128)S(1)} %get-tuple-element.219, f32[16,2,256]{2,0,1:T(8,128)S(1)} %get-tuple-element.220, f32[16,2,256]{2,0,1:T(8,128)S(1)} %get-tuple-element.221, s32[16,2,256]{2,0,1:T(8,128)S(1)} %get-tuple-element.222, ...), kind=kLoop, calls=%fused_computation.8.clone.1 | loop fusion | flops 46137344 | bytes 2883584 | tf_op jit(solution)/shard_map/while/body/eval_jaxpr/convert_element_type | solution.py:40
  321.1 7.4 scatter_fusion
  333.8 27.9 %add_convert_fusion.2 = bf16[16,2,256,128]{3,2,0,1:T(8,128)(2,1)S(1)} fusion(f32[16,2,256]{2,0,1:T(8,128)S(1)} %get-tuple-element.218, f32[16,2,256]{2,0,1:T(8,128)S(1)} %get-tuple-element.219, f32[16,2,256]{2,0,1:T(8,128)S(1)} %get-tuple-element.220, f32[16,2,256]{2,0,1:T(8,128)S(1)} %get-tuple-element.221, s32[16,2,256]{2,0,1:T(8,128)S(1)} %get-tuple-element.222, ...), kind=kLoop, calls=%fused_computation.8.clone.1 | loop fusion | flops 46137344 | bytes 2883584 | tf_op jit(solution)/shard_map/while/body/eval_jaxpr/convert_element_type | solution.py:40
  365.3 7.3 scatter_fusion
  377.8 27.9 %add_convert_fusion.2 = bf16[16,2,256,128]{3,2,0,1:T(8,128)(2,1)S(1)} fusion(f32[16,2,256]{2,0,1:T(8,128)S(1)} %get-tuple-element.218, f32[16,2,256]{2,0,1:T(8,128)S(1)} %get-tuple-element.219, f32[16,2,256]{2,0,1:T(8,128)S(1)} %get-tuple-element.220, f32[16,2,256]{2,0,1:T(8,128)S(1)} %get-tuple-element.221, s32[16,2,256]{2,0,1:T(8,128)S(1)} %get-tuple-element.222, ...), kind=kLoop, calls=%fused_computation.8.clone.1 | loop fusion | flops 46137344 | bytes 2883584 | tf_op jit(solution)/shard_map/while/body/eval_jaxpr/convert_element_type | solution.py:40
  409.4 7.5 scatter_fusion
  422.1 27.9 %add_convert_fusion.2 = bf16[16,2,256,128]{3,2,0,1:T(8,128)(2,1)S(1)} fusion(f32[16,2,256]{2,0,1:T(8,128)S(1)} %get-tuple-element.218, f32[16,2,256]{2,0,1:T(8,128)S(1)} %get-tuple-element.219, f32[16,2,256]{2,0,1:T(8,128)S(1)} %get-tuple-element.220, f32[16,2,256]{2,0,1:T(8,128)S(1)} %get-tuple-element.221, s32[16,2,256]{2,0,1:T(8,128)S(1)} %get-tuple-element.222, ...), kind=kLoop, calls=%fused_computation.8.clone.1 | loop fusion | flops 46137344 | bytes 2883584 | tf_op jit(solution)/shard_map/while/body/eval_jaxpr/convert_element_type | solution.py:40
  453.7 7.1 scatter_fusion
  466.0 27.9 %add_convert_fusion.2 = bf16[16,2,256,128]{3,2,0,1:T(8,128)(2,1)S(1)} fusion(f32[16,2,256]{2,0,1:T(8,128)S(1)} %get-tuple-element.218, f32[16,2,256]{2,0,1:T(8,128)S(1)} %get-tuple-element.219, f32[16,2,256]{2,0,1:T(8,128)S(1)} %get-tuple-element.220, f32[16,2,256]{2,0,1:T(8,128)S(1)} %get-tuple-element.221, s32[16,2,256]{2,0,1:T(8,128)S(1)} %get-tuple-element.222, ...), kind=kLoop, calls=%fused_computation.8.clone.1 | loop fusion | flops 46137344 | bytes 2883584 | tf_op jit(solution)/shard_map/while/body/eval_jaxpr/convert_element_type | solution.py:40
  497.6 7.7 scatter_fusion
  505.3 3.9 scatter_fusion.1
  510.9 27.9 %add_convert_fusion.2 = bf16[16,2,256,128]{3,2,0,1:T(8,128)(2,1)S(1)} fusion(f32[16,2,256]{2,0,1:T(8,128)S(1)} %get-tuple-element.218, f32[16,2,256]{2,0,1:T(8,128)S(1)} %get-tuple-element.219, f32[16,2,256]{2,0,1:T(8,128)S(1)} %get-tuple-element.220, f32[16,2,256]{2,0,1:T(8,128)S(1)} %get-tuple-element.221, s32[16,2,256]{2,0,1:T(8,128)S(1)} %get-tuple-element.222, ...), kind=kLoop, calls=%fused_computation.8.clone.1 | loop fusion | flops 46137344 | bytes 2883584 | tf_op jit(solution)/shard_map/while/body/eval_jaxpr/convert_element_type | solution.py:40
  542.5 7.4 scatter_fusion
  555.1 27.9 %add_convert_fusion.2 = bf16[16,2,256,128]{3,2,0,1:T(8,128)(2,1)S(1)} fusion(f32[16,2,256]{2,0,1:T(8,128)S(1)} %get-tuple-element.218, f32[16,2,256]{2,0,1:T(8,128)S(1)} %get-tuple-element.219, f32[16,2,256]{2,0,1:T(8,128)S(1)} %get-tuple-element.220, f32[16,2,256]{2,0,1:T(8,128)S(1)} %get-tuple-element.221, s32[16,2,256]{2,0,1:T(8,128)S(1)} %get-tuple-element.222, ...), kind=kLoop, calls=%fused_computation.8.clone.1 | loop fusion | flops 46137344 | bytes 2883584 | tf_op jit(solution)/shard_map/while/body/eval_jaxpr/convert_element_type | solution.py:40
  586.7 7.7 scatter_fusion
  594.4 3.9 scatter_fusion.1
  600.0 27.9 %add_convert_fusion.2 = bf16[16,2,256,128]{3,2,0,1:T(8,128)(2,1)S(1)} fusion(f32[16,2,256]{2,0,1:T(8,128)S(1)} %get-tuple-element.218, f32[16,2,256]{2,0,1:T(8,128)S(1)} %get-tuple-element.219, f32[16,2,256]{2,0,1:T(8,128)S(1)} %get-tuple-element.220, f32[16,2,256]{2,0,1:T(8,128)S(1)} %get-tuple-element.221, s32[16,2,256]{2,0,1:T(8,128)S(1)} %get-tuple-element.222, ...), kind=kLoop, calls=%fused_computation.8.clone.1 | loop fusion | flops 46137344 | bytes 2883584 | tf_op jit(solution)/shard_map/while/body/eval_jaxpr/convert_element_type | solution.py:40
  631.6 7.4 scatter_fusion
  644.1 27.9 %add_convert_fusion.2 = bf16[16,2,256,128]{3,2,0,1:T(8,128)(2,1)S(1)} fusion(f32[16,2,256]{2,0,1:T(8,128)S(1)} %get-tuple-element.218, f32[16,2,256]{2,0,1:T(8,128)S(1)} %get-tuple-element.219, f32[16,2,256]{2,0,1:T(8,128)S(1)} %get-tuple-element.220, f32[16,2,256]{2,0,1:T(8,128)S(1)} %get-tuple-element.221, s32[16,2,256]{2,0,1:T(8,128)S(1)} %get-tuple-element.222, ...), kind=kLoop, calls=%fused_computation.8.clone.1 | loop fusion | flops 46137344 | bytes 2883584 | tf_op jit(solution)/shard_map/while/body/eval_jaxpr/convert_element_type | solution.py:40
  675.7 7.7 scatter_fusion
  683.4 3.9 scatter_fusion.1
  689.0 27.9 %add_convert_fusion.2 = bf16[16,2,256,128]{3,2,0,1:T(8,128)(2,1)S(1)} fusion(f32[16,2,256]{2,0,1:T(8,128)S(1)} %get-tuple-element.218, f32[16,2,256]{2,0,1:T(8,128)S(1)} %get-tuple-element.219, f32[16,2,256]{2,0,1:T(8,128)S(1)} %get-tuple-element.220, f32[16,2,256]{2,0,1:T(8,128)S(1)} %get-tuple-element.221, s32[16,2,256]{2,0,1:T(8,128)S(1)} %get-tuple-element.222, ...), kind=kLoop, calls=%fused_computation.8.clone.1 | loop fusion | flops 46137344 | bytes 2883584 | tf_op jit(solution)/shard_map/while/body/eval_jaxpr/convert_element_type | solution.py:40
  720.6 7.5 scatter_fusion
  733.2 27.9 %add_convert_fusion.2 = bf16[16,2,256,128]{3,2,0,1:T(8,128)(2,1)S(1)} fusion(f32[16,2,256]{2,0,1:T(8,128)S(1)} %get-tuple-element.218, f32[16,2,256]{2,0,1:T(8,128)S(1)} %get-tuple-element.219, f32[16,2,256]{2,0,1:T(8,128)S(1)} %get-tuple-element.220, f32[16,2,256]{2,0,1:T(8,128)S(1)} %get-tuple-element.221, s32[16,2,256]{2,0,1:T(8,128)S(1)} %get-tuple-element.222, ...), kind=kLoop, calls=%fused_computation.8.clone.1 | loop fusion | flops 46137344 | bytes 2883584 | tf_op jit(solution)/shard_map/while/body/eval_jaxpr/convert_element_type | solution.py:40
  764.7 7.4 scatter_fusion
  777.4 27.9 %add_convert_fusion.2 = bf16[16,2,256,128]{3,2,0,1:T(8,128)(2,1)S(1)} fusion(f32[16,2,256]{2,0,1:T(8,128)S(1)} %get-tuple-element.218, f32[16,2,256]{2,0,1:T(8,128)S(1)} %get-tuple-element.219, f32[16,2,256]{2,0,1:T(8,128)S(1)} %get-tuple-element.220, f32[16,2,256]{2,0,1:T(8,128)S(1)} %get-tuple-element.221, s32[16,2,256]{2,0,1:T(8,128)S(1)} %get-tuple-element.222, ...), kind=kLoop, calls=%fused_computation.8.clone.1 | loop fusion | flops 46137344 | bytes 2883584 | tf_op jit(solution)/shard_map/while/body/eval_jaxpr/convert_element_type | solution.py:40
  808.9 7.4 scatter_fusion
  821.5 27.9 %add_convert_fusion.2 = bf16[16,2,256,128]{3,2,0,1:T(8,128)(2,1)S(1)} fusion(f32[16,2,256]{2,0,1:T(8,128)S(1)} %get-tuple-element.218, f32[16,2,256]{2,0,1:T(8,128)S(1)} %get-tuple-element.219, f32[16,2,256]{2,0,1:T(8,128)S(1)} %get-tuple-element.220, f32[16,2,256]{2,0,1:T(8,128)S(1)} %get-tuple-element.221, s32[16,2,256]{2,0,1:T(8,128)S(1)} %get-tuple-element.222, ...), kind=kLoop, calls=%fused_computation.8.clone.1 | loop fusion | flops 46137344 | bytes 2883584 | tf_op jit(solution)/shard_map/while/body/eval_jaxpr/convert_element_type | solution.py:40
  853.1 7.2 scatter_fusion
  870.4 4.4 collective-permute-done
  (429 shorter events, 154.1 us)
Async XLA Ops:
  4.0 14.4 %all-to-all-start = ((s32[32,8,1]{1,2,0:T(1,128)}), s32[32,8,1]{1,2,0:T(1,128)S(1)}, u32[]{:S(2)}, u32[]{:S(2)}) async-start(s32[32,8,1]{1,2,0:T(1,128)} %bitcast.34), calls=%async_computation | async-start | bytes 32768 | tf_op jit(solution)/shard_map/all_to_all | solution.py:70
  18.4 27.7 %copy-start.5 = (bf16[128,2,4,256]{3,2,1,0:T(4,128)(2,1)S(1)}, bf16[128,2,4,256]{3,2,1,0:T(4,128)(2,1)}, u32[]{:S(2)}) copy-start(bf16[128,2,4,256]{3,2,1,0:T(4,128)(2,1)} %param.13) | copy-start | bytes 1572868
  18.4 20.4 %all-to-all-start.4 = ((bf16[32,8,256]{2,1,0:T(8,128)(2,1)}), bf16[32,8,256]{2,1,0:T(8,128)(2,1)S(1)}, u32[]{:S(2)}, u32[]{:S(2)}) async-start(bf16[32,8,256]{2,1,0:T(8,128)(2,1)} %bitcast.38), calls=%async_computation.4 | async-start | bytes 262144 | tf_op jit(solution)/shard_map/all_to_all | solution.py:69
  38.8 32.2 %all-to-all-start.1 = ((bf16[256,2,4,256]{3,2,1,0:T(4,128)(2,1)}), bf16[256,2,4,256]{3,2,1,0:T(4,128)(2,1)}, u32[]{:S(2)}, u32[]{:S(2)}) async-start(bf16[256,2,4,256]{3,2,1,0:T(4,128)(2,1)} %scatter_fusion.3), calls=%async_computation.1 | async-start | bytes 2097152 | tf_op jit(solution)/shard_map/all_to_all | solution.py:68
  46.1 30.3 %copy-start.4 = (s32[128,2,4,256]{3,2,1,0:T(4,128)S(1)}, s32[128,2,4,256]{3,2,1,0:T(4,128)}, u32[]{:S(2)}) copy-start(s32[128,2,4,256]{3,2,1,0:T(4,128)} %param.12) | copy-start | bytes 3145732
  71.0 30.0 %all-to-all-start.3 = ((bf16[256,2,4,256]{3,2,1,0:T(4,128)(2,1)}), bf16[256,2,4,256]{3,2,1,0:T(4,128)(2,1)}, u32[]{:S(2)}, u32[]{:S(2)}) async-start(bf16[256,2,4,256]{3,2,1,0:T(4,128)(2,1)} %scatter_fusion.5), calls=%async_computation.3 | async-start | bytes 2097152 | tf_op jit(solution)/shard_map/all_to_all | solution.py:67
  101.0 52.5 %all-to-all-start.2 = ((s32[256,2,4,256]{3,2,1,0:T(4,128)}), s32[256,2,4,256]{3,2,1,0:T(4,128)S(1)}, u32[]{:S(2)}, u32[]{:S(2)}) async-start(s32[256,2,4,256]{3,2,1,0:T(4,128)} %scatter_fusion.4), calls=%async_computation.2 | async-start | bytes 4194304 | tf_op jit(solution)/shard_map/all_to_all | solution.py:66
  155.5 1.7 copy-start.1
  196.2 3.6 copy-start.2
  199.7 1.7 copy-start.1
  240.2 3.5 copy-start.2
  243.7 1.7 copy-start.1
  284.3 3.5 copy-start.2
  287.8 1.7 copy-start.1
  328.5 3.6 copy-start.2
  332.1 1.7 copy-start.1
  372.7 3.5 copy-start.2
  376.1 1.7 copy-start.1
  416.9 3.5 copy-start.2
  420.4 1.7 copy-start.1
  460.8 3.5 copy-start.2
  464.3 1.7 copy-start.1
  505.3 3.9 copy-start.2
  509.2 1.7 copy-start.1
  549.9 3.5 copy-start.2
  553.4 1.7 copy-start.1
  594.4 3.9 copy-start.2
  598.3 1.7 copy-start.1
  639.0 3.4 copy-start.2
  642.4 1.7 copy-start.1
  683.4 3.9 copy-start.2
  687.3 1.7 copy-start.1
  728.1 3.4 copy-start.2
  731.5 1.7 copy-start.1
  772.1 3.5 copy-start.2
  775.7 1.7 copy-start.1
  816.3 3.5 copy-start.2
  819.8 1.7 copy-start.1
  860.3 3.5 copy-start.2
  863.8 6.6 collective-permute-start.1
  866.8 8.0 collective-permute-start
  870.4 5.3 copy-start
  875.7 1.6 copy-start.3
where the time goes:
time: 882 us; the launch traced here: 877 us
  other arithmetic  640 us (73%)
  local copies, waits for them, and re-layouts  81.8 us (9%)
  waiting for transfers between devices  80.4 us (9%)
  matrix products  47 us (5%)
  starting transfers between devices  25.1 us (3%)
    convert_element_type x16, other arithmetic, basis_tiles(): return summed.astype(jnp.bfloat16)  446 us
    scatter-add x32, other arithmetic, accumulate(): band_acc = band_acc.at[rows_at, band_lag].add(products)  176 us
    scatter x5, local copies, waits for them, and re-layouts, place(): return empty.at[target].set(values)  47.6 us
    all_to_all x1, waiting for transfers between devices, on_device(): lax.all_to_all(send_index, ('frame', 'panel'), split_axis=0, concat_axis=...  47.5 us
    dot_general x32, matrix products, accumulate(): jnp.einsum('bsxi,bsxj->bsij', left_tiles, right_tiles, preferred_element_...  40.9 us
    dynamic_slice x80, local copies, waits for them, and re-layouts, on_device(): lax.scan(accumulate, (band_init, rhs_init), (split(incoming[0]), split(in...  18.8 us
  transfers between devices with their start and end apart: 7, of which 6 were waited for; matrix products, arithmetic and copies ran while one was open for 6% of the time, Pallas kernels for 0%

commit v1 on v0

v1 whole, which is shorter than its diff:
```python
import functools

import jax
import jax.numpy as jnp
from jax import lax
from jax.experimental import pallas as pl
from jax.experimental.pallas import tpu as pltpu
from jax.sharding import PartitionSpec as P

CO = 128
BLK_DEV = 22
PARTS = 1
GROUP = 16
ACC_ROWS = BLK_DEV + 3
TRASH = BLK_DEV + 1
HEAD = 16
AXES = ("frame", "panel")


def normal_kernel(terms, width, where_ref, rows_ref, *refs):
    if len(refs) == 12:
        band_in, rhs_in = refs[:2]
        refs = refs[2:]
    else:
        band_in = rhs_in = None
    band_ref, rhs_ref, index_ref, weight_ref, force_ref, even_ref, odd_ref, list_ref, block_ref = refs[:9]
    slots = rows_ref.shape[0]
    span = terms * width
    lanes = width // 128
    neighbors = terms // 2

    if band_in is None:
        band_ref[...] = jnp.zeros_like(band_ref)
        rhs_ref[...] = jnp.zeros_like(rhs_ref)
    else:
        band_ref[...] = band_in[...]
        rhs_ref[...] = rhs_in[...]

    def gather_list(slot, count):
        filled = where_ref[slot]
        list_ref[count] = slot
        block_ref[count] = filled - 1
        return count + (filled > 0).astype(jnp.int32)

    count = lax.fori_loop(0, slots, gather_list, jnp.int32(0))
    list_ref[count] = 0
    block_ref[count] = TRASH

    @pl.loop(0, slots // GROUP)
    def dense(group):
        at = pl.ds(pl.multiple_of(group * GROUP, GROUP), GROUP)
        for col in range(span // 128):
            index_ref[col, at, :] = rows_ref[at, pl.ds(col * 128, 128)].astype(jnp.float32).astype(jnp.int32)
            t = rows_ref[at, pl.ds(span + col * 128, 128)].astype(jnp.float32)
            p = rows_ref[at, pl.ds(2 * span + col * 128, 128)].astype(jnp.float32) * (1.0 / 6.0)
            one = 1.0 - t
            square = t * t
            cube = square * t
            weight_ref[0, col, at, :] = p * (one * one * one)
            weight_ref[1, col, at, :] = p * (3.0 * cube - 6.0 * square + 4.0)
            weight_ref[2, col, at, :] = p * (3.0 * (square - cube + t) + 1.0)
            weight_ref[3, col, at, :] = p * cube
        for lane in range(lanes):
            force_ref[lane, at, :] = rows_ref[at, pl.ds(3 * span + lane * 128, 128)].astype(jnp.float32)

    sub = lax.broadcasted_iota(jnp.int32, (8, 128), 0)

    def build(slot, design_ref):
        at = pl.ds(slot, 1)
        for lane in range(lanes):
            force = jnp.broadcast_to(force_ref[lane, at, :], (HEAD, 128)).astype(jnp.bfloat16)
            design_ref[0:HEAD, lane * 128 : lane * 128 + 128] = force
        for s in range(2):
            for lane in range(lanes):
                tiles = [None] * (CO // 8)
                for n in range(neighbors):
                    col = (s * neighbors + n) * lanes + lane
                    index = jnp.broadcast_to(index_ref[col, at, :], (8, 128))
                    m = (sub - index) & 7
                    value = jnp.where(m == 3, jnp.broadcast_to(weight_ref[3, col, at, :], (8, 128)), 0.0)
                    for k in (2, 1, 0):
                        value = jnp.where(m == k, jnp.broadcast_to(weight_ref[k, col, at, :], (8, 128)), value)
                    target = (index + m) >> 3
                    for a in range(CO // 8):
                        part = jnp.where(target == a, value, 0.0)
                        tiles[a] = part if tiles[a] is None else tiles[a] + part
                for a in range(0, CO // 8, 2):
                    pair = jnp.concatenate([tiles[a], tiles[a + 1]], axis=0).astype(jnp.bfloat16)
                    design_ref[HEAD + s * CO + a * 8 : HEAD + s * CO + a * 8 + 16, lane * 128 : lane * 128 + 128] = pair

    contract = (((1,), (1,)), ((), ()))

    def add(block, design_ref):
        top = lax.dot_general(
            design_ref[0 : HEAD + CO, :], design_ref[HEAD:, :], contract, preferred_element_type=jnp.float32
        )
        low = lax.dot_general(
            design_ref[HEAD + CO :, :], design_ref[HEAD + CO :, :], contract, preferred_element_type=jnp.float32
        )
        band_ref[block, 0] += top[HEAD:, :CO]
        band_ref[block, 1] += top[HEAD:, CO:]
        band_ref[block + 1, 0] += low
        rhs_ref[block] += top[0:8, :CO]
        rhs_ref[block + 1] += top[0:8, CO:]

    odd_ref[...] = jnp.zeros_like(odd_ref)

    def pair(step, before):
        first = 2 * step
        build(list_ref[first], even_ref)
        add(before, odd_ref)
        build(list_ref[first + 1], odd_ref)
        add(block_ref[first], even_ref)
        return block_ref[first + 1]

    last = lax.fori_loop(0, (count + 1) // 2, pair, jnp.int32(TRASH))
    add(last, odd_ref)


def normal_sums(where, rows, terms, width, totals):
    slots = rows.shape[0]
    span = terms * width
    vmem = pl.BlockSpec(memory_space=pltpu.VMEM)
    smem = pl.BlockSpec(memory_space=pltpu.SMEM)
    carried = () if totals is None else totals
    return pl.pallas_call(
        functools.partial(normal_kernel, terms, width),
        out_shape=(
            jax.ShapeDtypeStruct((ACC_ROWS, 2, CO, CO), jnp.float32),
            jax.ShapeDtypeStruct((ACC_ROWS, 8, CO), jnp.float32),
        ),
        in_specs=[smem, vmem] + [vmem] * len(carried),
        out_specs=(vmem, vmem),
        scratch_shapes=[
            pltpu.VMEM((span // 128, slots, 128), jnp.int32),
            pltpu.VMEM((4, span // 128, slots, 128), jnp.float32),
            pltpu.VMEM((width // 128, slots, 128), jnp.float32),
            pltpu.VMEM((HEAD + 2 * CO, width), jnp.bfloat16),
            pltpu.VMEM((HEAD + 2 * CO, width), jnp.bfloat16),
            pltpu.SMEM((slots + 8,), jnp.int32),
            pltpu.SMEM((slots + 8,), jnp.int32),
        ],
        compiler_params=pltpu.CompilerParams(vmem_limit_bytes=40 * 1024 * 1024),
        cost_estimate=pl.CostEstimate(
            flops=slots * 20 * 1000 * 1000 * width // 256, bytes_accessed=10 * 1000 * 1000, transcendentals=0
        ),
    )(where, rows, *carried)


def on_device(spline_index, spline_frac, projection, forces, row_owner, row_offset):
    row_count, slot_width, neighbors, design_rows = spline_index.shape
    terms = slot_width * neighbors
    device_count = lax.axis_size(AXES)
    capacity = max(2, 2 * row_count // device_count)
    slot_count = device_count * capacity
    width = design_rows // PARTS

    owners = row_owner[:, 0]
    same_owner = owners[:, None] == owners[None, :]
    row_at = lax.broadcasted_iota(jnp.int32, (row_count, row_count), 0)
    other_at = lax.broadcasted_iota(jnp.int32, (row_count, row_count), 1)
    position = jnp.sum((same_owner & (other_at < row_at)).astype(jnp.int32), axis=1)
    target = owners * capacity + position
    chosen = (lax.broadcasted_iota(jnp.int32, (slot_count, row_count), 0) == target[None, :]).astype(jnp.bfloat16)
    tag = jnp.broadcast_to((row_offset + 1).astype(jnp.bfloat16)[:, None], (row_count, 128))

    received = []
    for part in range(PARTS):
        cut = slice(part * width, (part + 1) * width)
        payload = jnp.concatenate(
            [
                spline_index[..., cut].astype(jnp.bfloat16).reshape(row_count, terms * width),
                spline_frac[..., cut].reshape(row_count, terms * width),
                projection[..., cut].reshape(row_count, terms * width),
                forces[:, cut],
                tag,
            ],
            axis=1,
        )
        outgoing = jnp.dot(chosen, payload, preferred_element_type=jnp.bfloat16)
        received.append(lax.all_to_all(outgoing, AXES, split_axis=0, concat_axis=0, tiled=True))

    totals = None
    for rows in received:
        where = rows[:, 3 * terms * width + width].astype(jnp.int32)
        totals = normal_sums(where, rows, terms, width, totals)
    band, rhs = totals
    rhs = rhs[:, 0]
    spill = jnp.concatenate([band[BLK_DEV, 0], rhs[BLK_DEV : BLK_DEV + 1]], axis=0)
    route = [(i, (i + 1) % device_count) for i in range(device_count)]
    spill = lax.ppermute(spill, AXES, route)
    normal_band = band[:BLK_DEV].at[0, 0].add(spill[:CO])
    normal_rhs = rhs[:BLK_DEV].at[0].add(spill[CO])
    return (normal_band, normal_rhs)


def solution(mesh):
    split = P(AXES)
    return jax.shard_map(
        on_device, mesh=mesh, in_specs=(split,) * 6, out_specs=(split, split), check_vma=False
    )
```

time: 882 us -> 135 us (0.15)
  other arithmetic: 640 us -> 4.51 us
  blocking collectives: 0 us -> 84 us
  local copies, waits for them, and re-layouts: 81.8 us -> 3.87 us
  waiting for transfers between devices: 80.4 us -> 5.53 us
  matrix products: 47 us -> 1.01 us
  Pallas kernels: 0 us -> 34.6 us
  starting transfers between devices: 25.1 us -> 0.06 us
    convert_element_type x32 -> x3, other arithmetic: 447 us -> 2.3 us  [the longest x1 1.46 us: on_device(): spline_index[..., cut].astype(jnp.bfloat16)]
    scatter-add x49 -> x1, other arithmetic: 188 us -> 0.64 us  [on_device(): normal_band = band[:BLK_DEV].at[0, 0].add(spill[:CO])]
    all_to_all x0 -> x1, blocking collectives: none -> 84 us  [on_device(): lax.all_to_all(outgoing, AXES, split_axis=0, concat_axis=0, tiled=True)]
    all_to_all x5 -> x0, waiting for transfers between devices: 74.1 us -> none  [the longest x1 47.5 us: on_device(): lax.all_to_all(send_index, ('frame', 'panel'), split_axis=0, concat_axis=...]
    scatter x5 -> x0, local copies, waits for them, and re-layouts: 47.6 us -> none  [place(): return empty.at[target].set(values)]
    dot_general x48 -> x1, matrix products: 47 us -> 1.01 us  [on_device(): outgoing = jnp.dot(chosen, payload, preferred_element_type=jnp.bfloat16)]
    pallas_call x0 -> x1, Pallas kernels: none -> 34.6 us  [normal_sums(): pl.pallas_call(functools.partial(normal_kernel, terms, width), out_shape=...]
    all_to_all x5 -> x0, starting transfers between devices: 23.3 us -> none  [the longest x1 7.3 us: on_device(): lax.all_to_all(send_offset, ('frame', 'panel'), split_axis=0, concat_axis...]
  transfers between devices with their start and end apart: 7 -> 1, of which waited for: 6 -> 1; matrix products, arithmetic and copies ran while one was open for 6% -> 1% of each run, Pallas kernels for 0% -> 0%
where the time goes in v1:
time: 135 us; the launch traced here: 134 us
  blocking collectives  84 us (62%)
  Pallas kernels  34.6 us (26%)
  waiting for transfers between devices  5.53 us (4%)
  other arithmetic  4.51 us (3%)
  local copies, waits for them, and re-layouts  3.87 us (3%)
    all_to_all x1, blocking collectives, on_device(): lax.all_to_all(outgoing, AXES, split_axis=0, concat_axis=0, tiled=True)  84 us
    pallas_call x1, Pallas kernels, normal_sums(): pl.pallas_call(functools.partial(normal_kernel, terms, width), out_shape=...  34.6 us
    ppermute x1, waiting for transfers between devices, on_device(): spill = lax.ppermute(spill, AXES, route)  5.53 us
  transfers between devices with their start and end apart: 1, of which 1 were waited for; matrix products, arithmetic and copies ran while one was open for 1% of the time, Pallas kernels for 0%

profile of v1, /device:TPU:0, one launch (start us, length us, event | category | flops | bytes accessed | tf_op | source)
XLA Modules:
  0.0 134.3 jit_solution(2710487877481821539)
XLA Ops:
  0.6 0.0 copy-start
  0.6 0.7 add_convert_fusion
  1.4 0.9 convert_reduce_fusion.1
  2.3 0.7 multiply_add_fusion
  2.9 0.0 copy-start.1
  2.9 1.5 %convert_element_type.16 = bf16[128,2,4,256]{3,2,1,0:T(4,128)(2,1)S(1)} convert(s32[128,2,4,256]{3,2,1,0:T(4,128)} %param.10) | non-fusion elementwise | flops 262144 | bytes 1572864 | tf_op jit(solution)/shard_map/convert_element_type | solution.py:172
  4.4 0.4 reshape.95
  4.8 0.0 copy-done
  4.8 0.4 reshape.96
  5.2 0.0 copy-done.1
  5.2 0.4 reshape.97
  5.6 0.0 copy-start.2
  5.7 0.7 copy-done.2
  6.4 0.1 broadcast_dynamic-update-slice_fusion
  6.5 1.0 convolution_bitcast_fusion
  7.5 84.0 %all_to_all.11 = bf16[32,8,6528]{2,1,0:T(8,128)(2,1)S(1)} all-to-all(bf16[32,8,6528]{2,1,0:T(8,128)(2,1)S(1)} %convolution_bitcast_fusion), channel_id=1, replica_groups=mesh['frame'=4,'panel'=8] {'frame','panel'}, dimensions={0} | all-to-all | bytes 6684672 | tf_op jit(solution)/shard_map/all_to_all | solution.py:181
  91.5 0.1 convert_reduce_fusion.where_ref
  91.6 34.6 %shard_map.77 = (f32[25,2,128,128]{3,2,1,0:T(8,128)S(1)}, f32[25,8,128]{2,1,0:T(8,128)S(1)}) custom-call(s32[256]{0:T(256)S(1)} %convert_reduce_fusion.where_ref, bf16[256,6528]{1,0:T(8,128)(2,1)S(1)} %bitcast.22), custom_call_target="tpu_custom_call" | custom-call | flops 5120000000 | bytes 10000000 | tf_op jit(solution)/shard_map/pallas_call | solution.py:126
  126.3 0.1 collective-permute-start
  126.4 1.8 %slice.79 = f32[22,2,128,128]{3,2,1,0:T(8,128)} slice(f32[25,2,128,128]{3,2,1,0:T(8,128)S(1)} %get-tuple-element.28), slice={[0:22], [0:2], [0:128], [0:128]} | slice | bytes 5767168 | tf_op jit(solution)/shard_map/slice | solution.py:192
  128.1 5.5 %collective-permute-done = f32[129,128]{1,0:T(8,128)S(1)} collective-permute-done((f32[129,128]{1,0:T(8,128)S(1)}, f32[129,128]{1,0:T(8,128)S(1)}, u32[]{:S(2)}, u32[]{:S(2)}) %collective-permute-start) | collective-permute-done | bytes 66080 | tf_op jit(solution)/shard_map/ppermute | solution.py:191
  133.7 0.0 copy-start.3
  133.7 0.6 fusion.1
  134.3 0.0 copy-done.3
  (11 shorter events, 0.2 us)
Async XLA Ops:
  0.6 4.2 %copy-start = (bf16[128,2,4,256]{3,2,1,0:T(4,128)(2,1)S(1)}, bf16[128,2,4,256]{3,2,1,0:T(4,128)(2,1)}, u32[]{:S(2)}) copy-start(bf16[128,2,4,256]{3,2,1,0:T(4,128)(2,1)} %param.11) | copy-start | bytes 1572868
  2.9 2.2 %copy-start.1 = (bf16[128,2,4,256]{3,2,1,0:T(4,128)(2,1)S(1)}, bf16[128,2,4,256]{3,2,1,0:T(4,128)(2,1)}, u32[]{:S(2)}) copy-start(bf16[128,2,4,256]{3,2,1,0:T(4,128)(2,1)} %param.12) | copy-start | bytes 1572868
  5.6 0.8 copy-start.2
  126.3 7.4 %collective-permute-start = (f32[129,128]{1,0:T(8,128)S(1)}, f32[129,128]{1,0:T(8,128)S(1)}, u32[]{:S(2)}, u32[]{:S(2)}) collective-permute-start(f32[129,128]{1,0:T(8,128)S(1)} %pad_maximum_fusion), channel_id=1, source_target_pairs={{0,1},{1,2},{2,3},{3,4},{4,5},{5,6},{6,7},{7,8},{8,9},{9,10},{10,1... | collective-permute-start | bytes 198152 | tf_op jit(solution)/shard_map/ppermute | solution.py:191
  133.7 0.6 copy-start.3

commit v2 on v1

--- a/solution.py
+++ b/solution.py
@@ -9,7 +9,6 @@
 
 CO = 128
 BLK_DEV = 22
-PARTS = 1
 GROUP = 16
 ACC_ROWS = BLK_DEV + 3
 TRASH = BLK_DEV + 1
@@ -18,12 +17,12 @@
 
 
 def normal_kernel(terms, width, where_ref, rows_ref, *refs):
-    if len(refs) == 12:
+    if len(refs) == 11:
         band_in, rhs_in = refs[:2]
         refs = refs[2:]
     else:
         band_in = rhs_in = None
-    band_ref, rhs_ref, index_ref, weight_ref, force_ref, even_ref, odd_ref, list_ref, block_ref = refs[:9]
+    band_ref, rhs_ref, index_ref, weight_ref, force_ref, even_ref, odd_ref, list_ref, block_ref = refs
     slots = rows_ref.shape[0]
     span = terms * width
     lanes = width // 128
@@ -152,33 +151,34 @@
     terms = slot_width * neighbors
     device_count = lax.axis_size(AXES)
     capacity = max(2, 2 * row_count // device_count)
-    slot_count = device_count * capacity
-    width = design_rows // PARTS
+    width = design_rows
+    waves = [size for size in (capacity // 2, capacity // 4, capacity - capacity // 2 - capacity // 4) if size]
 
     owners = row_owner[:, 0]
     same_owner = owners[:, None] == owners[None, :]
     row_at = lax.broadcasted_iota(jnp.int32, (row_count, row_count), 0)
     other_at = lax.broadcasted_iota(jnp.int32, (row_count, row_count), 1)
     position = jnp.sum((same_owner & (other_at < row_at)).astype(jnp.int32), axis=1)
-    target = owners * capacity + position
-    chosen = (lax.broadcasted_iota(jnp.int32, (slot_count, row_count), 0) == target[None, :]).astype(jnp.bfloat16)
     tag = jnp.broadcast_to((row_offset + 1).astype(jnp.bfloat16)[:, None], (row_count, 128))
+    payload = jnp.concatenate(
+        [
+            spline_index.astype(jnp.bfloat16).reshape(row_count, terms * width),
+            spline_frac.reshape(row_count, terms * width),
+            projection.reshape(row_count, terms * width),
+            forces,
+            tag,
+        ],
+        axis=1,
+    )
 
     received = []
-    for part in range(PARTS):
-        cut = slice(part * width, (part + 1) * width)
-        payload = jnp.concatenate(
-            [
-                spline_index[..., cut].astype(jnp.bfloat16).reshape(row_count, terms * width),
-                spline_frac[..., cut].reshape(row_count, terms * width),
-                projection[..., cut].reshape(row_count, terms * width),
-                forces[:, cut],
-                tag,
-            ],
-            axis=1,
-        )
-        outgoing = jnp.dot(chosen, payload, preferred_element_type=jnp.bfloat16)
+    first = 0
+    for size in waves:
+        slot_at = lax.broadcasted_iota(jnp.int32, (device_count * size, row_count), 0)
+        chosen = (slot_at // size == owners[None, :]) & (slot_at % size + first == position[None, :])
+        outgoing = jnp.dot(chosen.astype(jnp.bfloat16), payload, preferred_element_type=jnp.bfloat16)
         received.append(lax.all_to_all(outgoing, AXES, split_axis=0, concat_axis=0, tiled=True))
+        first += size
 
     totals = None
     for rows in received:

time: 135 us -> 154 us (1.14)
  blocking collectives: 84 us -> 0 us
  waiting for transfers between devices: 5.53 us -> 80.9 us
  starting transfers between devices: 0.06 us -> 14.8 us
  local copies, waits for them, and re-layouts: 3.87 us -> 14 us
  Pallas kernels: 34.6 us -> 36.7 us
    all_to_all x1 -> x0, blocking collectives: 84 us -> none  [on_device(): lax.all_to_all(outgoing, AXES, split_axis=0, concat_axis=0, tiled=True)]
    all_to_all x0 -> x3, waiting for transfers between devices: none -> 75.3 us  [on_device(): lax.all_to_all(outgoing, AXES, split_axis=0, concat_axis=0, tiled=True)]
    all_to_all x0 -> x3, starting transfers between devices: none -> 14.8 us  [on_device(): lax.all_to_all(outgoing, AXES, split_axis=0, concat_axis=0, tiled=True)]
    all_to_all x0 -> x6, local copies, waits for them, and re-layouts: none -> 9.26 us  [on_device(): lax.all_to_all(outgoing, AXES, split_axis=0, concat_axis=0, tiled=True)]
    pallas_call x1 -> x3, Pallas kernels: 34.6 us -> 36.7 us  [normal_sums(): pl.pallas_call(functools.partial(normal_kernel, terms, width), out_shape=...]
  transfers between devices with their start and end apart: 1 -> 4, of which waited for: 1 -> 4; matrix products, arithmetic and copies ran while one was open for 1% -> 2% of each run, Pallas kernels for 0% -> 0%
where the time goes in v2:
time: 154 us; the launch traced here: 153 us
  waiting for transfers between devices  80.9 us (53%)
  Pallas kernels  36.7 us (24%)
  starting transfers between devices  14.8 us (10%)
  local copies, waits for them, and re-layouts  14 us (9%)
  other arithmetic  4.04 us (3%)
  matrix products  1.61 us (1%)
    all_to_all x3, waiting for transfers between devices, on_device(): lax.all_to_all(outgoing, AXES, split_axis=0, concat_axis=0, tiled=True)  75.3 us
    pallas_call x3, Pallas kernels, normal_sums(): pl.pallas_call(functools.partial(normal_kernel, terms, width), out_shape=...  36.7 us
    all_to_all x3, starting transfers between devices, on_device(): lax.all_to_all(outgoing, AXES, split_axis=0, concat_axis=0, tiled=True)  14.8 us
    all_to_all x6, local copies, waits for them, and re-layouts, on_device(): lax.all_to_all(outgoing, AXES, split_axis=0, concat_axis=0, tiled=True)  9.26 us
    ppermute x1, waiting for transfers between devices, on_device(): spill = lax.ppermute(spill, AXES, route)  5.53 us
  transfers between devices with their start and end apart: 4, of which 4 were waited for; matrix products, arithmetic and copies ran while one was open for 2% of the time, Pallas kernels for 0%

profile of v2, /device:TPU:0, one launch (start us, length us, event | category | flops | bytes accessed | tf_op | source)
XLA Modules:
  0.0 153.0 jit_solution(9970417965241464156)
XLA Ops:
  0.6 0.0 copy-start.4
  0.7 0.9 convert_reduce_fusion.1
  1.6 0.7 add_convert_fusion
  2.2 0.0 copy-start.5
  2.2 1.5 convert_element_type.28
  3.7 0.4 reshape.96
  4.1 0.0 copy-done.4
  4.1 0.4 reshape.97
  4.5 0.0 copy-done.5
  4.5 0.4 reshape.98
  4.9 0.0 copy-start.6
  4.9 0.0 copy-start.8
  5.0 0.7 copy-done.6
  5.7 0.1 broadcast_dynamic-update-slice_fusion
  5.8 0.0 copy-done.8
  5.8 0.5 fusion.18
  6.3 1.2 all_to_all.24
  7.5 7.3 %all-to-all-start.1 = ((bf16[32,2,6528]{2,1,0:T(2,128)(2,1)}), bf16[32,2,6528]{2,1,0:T(2,128)(2,1)S(1)}, u32[]{:S(2)}, u32[]{:S(2)}) async-start(bf16[32,2,6528]{2,1,0:T(2,128)(2,1)} %all_to_all.24), calls=%async_computation.1 | async-start | bytes 1671168 | tf_op jit(solution)/shard_map/all_to_all | solution.py:180
  14.8 0.5 fusion.20
  15.3 1.2 all_to_all.21
  16.5 20.0 %all-to-all-done.1 = bf16[32,2,6528]{2,1,0:T(2,128)(2,1)S(1)} async-done(((bf16[32,2,6528]{2,1,0:T(2,128)(2,1)}), bf16[32,2,6528]{2,1,0:T(2,128)(2,1)S(1)}, u32[]{:S(2)}, u32[]{:S(2)}) %all-to-all-start.1) | async-done | bytes 835616 | tf_op jit(solution)/shard_map/all_to_all | solution.py:180
  36.5 0.0 copy-start.2
  36.5 3.7 %all-to-all-start = ((bf16[32,2,6528]{2,1,0:T(2,128)(2,1)}), bf16[32,2,6528]{2,1,0:T(2,128)(2,1)}, u32[]{:S(2)}, u32[]{:S(2)}) async-start(bf16[32,2,6528]{2,1,0:T(2,128)(2,1)} %all_to_all.21), calls=%async_computation | async-start | bytes 1671168 | tf_op jit(solution)/shard_map/all_to_all | solution.py:180
  40.3 0.0 copy-done.2
  40.3 0.7 fusion.4
  41.0 1.4 all_to_all.27
  42.4 19.5 %all-to-all-done = bf16[32,2,6528]{2,1,0:T(2,128)(2,1)} async-done(((bf16[32,2,6528]{2,1,0:T(2,128)(2,1)}), bf16[32,2,6528]{2,1,0:T(2,128)(2,1)}, u32[]{:S(2)}, u32[]{:S(2)}) %all-to-all-start) | async-done | bytes 835616 | tf_op jit(solution)/shard_map/all_to_all | solution.py:180
  61.9 3.7 %all-to-all-start.2 = ((bf16[32,4,6528]{2,1,0:T(4,128)(2,1)}), bf16[32,4,6528]{2,1,0:T(4,128)(2,1)}, u32[]{:S(2)}, u32[]{:S(2)}) async-start(bf16[32,4,6528]{2,1,0:T(4,128)(2,1)} %all_to_all.27), calls=%async_computation.2 | async-start | bytes 3342336 | tf_op jit(solution)/shard_map/all_to_all | solution.py:180
  65.6 0.0 copy-done.3
  65.6 0.3 all_to_all.26.rows_ref
  66.0 2.4 %all_to_all.23.rows_ref = bf16[64,6528]{1,0:T(8,128)(2,1)S(1)} reshape(bf16[32,2,6528]{2,1,0:T(2,128)(2,1)} %all-to-all-done) | data formatting | bytes 1671168 | tf_op jit(solution)/shard_map/all_to_all | solution.py:180
  68.4 0.1 convert_reduce_fusion.2.where_ref
  68.5 0.1 convert_reduce_fusion.3.where_ref
  68.6 0.0 copy-start
  68.6 0.9 copy-done
  69.5 35.8 %all-to-all-done.2 = bf16[32,4,6528]{2,1,0:T(4,128)(2,1)} async-done(((bf16[32,4,6528]{2,1,0:T(4,128)(2,1)}), bf16[32,4,6528]{2,1,0:T(4,128)(2,1)}, u32[]{:S(2)}, u32[]{:S(2)}) %all-to-all-start.2) | async-done | bytes 1671200 | tf_op jit(solution)/shard_map/all_to_all | solution.py:180
  105.3 2.7 %all_to_all.29.rows_ref = bf16[128,6528]{1,0:T(8,128)(2,1)S(1)} reshape(bf16[32,4,6528]{2,1,0:T(4,128)(2,1)} %all-to-all-done.2) | data formatting | bytes 3342336 | tf_op jit(solution)/shard_map/all_to_all | solution.py:180
  108.1 0.1 convert_reduce_fusion.where_ref
  108.2 17.9 %shard_map.77 = (f32[25,2,128,128]{3,2,1,0:T(8,128)S(1)}, f32[25,8,128]{2,1,0:T(8,128)S(1)}) custom-call(s32[128]{0:T(128)S(1)} %convert_reduce_fusion.where_ref, bf16[128,6528]{1,0:T(8,128)(2,1)S(1)} %all_to_all.29.rows_ref), custom_call_target="tpu_custom_call" | custom-call | flops 2560000000 | bytes 10000000 | tf_op jit(solution)/shard_map/pallas_call | solution.py:125
  126.1 0.0 copy-start.1
  126.1 9.4 %shard_map.78 = (f32[25,2,128,128]{3,2,1,0:T(8,128)S(1)}, f32[25,8,128]{2,1,0:T(8,128)S(1)}) custom-call(s32[64]{0:T(128)S(1)} %convert_reduce_fusion.2.where_ref, bf16[64,6528]{1,0:T(8,128)(2,1)S(1)} %all_to_all.26.rows_ref, f32[25,2,128,128]{3,2,1,0:T(8,128)S(1)} %get-tuple-element.32.refs_0_, f32[25,8,128]{2,1,0:T(8,128)S(1)} %get-tuple-element.33.refs_1_), custom_call_target="tpu_custom_call" | custom-call | flops 1280000000 | bytes 10000000 | tf_op jit(solution)/shard_map/pallas_call | solution.py:125
  135.5 0.0 copy-done.1
  135.5 9.4 %shard_map.79 = (f32[25,2,128,128]{3,2,1,0:T(8,128)S(1)}, f32[25,8,128]{2,1,0:T(8,128)S(1)}) custom-call(s32[64]{0:T(128)S(1)} %convert_reduce_fusion.3.where_ref, bf16[64,6528]{1,0:T(8,128)(2,1)S(1)} %copy-done.1, f32[25,2,128,128]{3,2,1,0:T(8,128)S(1)} %get-tuple-element.34.refs_0_, f32[25,8,128]{2,1,0:T(8,128)S(1)} %get-tuple-element.35.refs_1_), custom_call_target="tpu_custom_call" | custom-call | flops 1280000000 | bytes 10000000 | tf_op jit(solution)/shard_map/pallas_call | solution.py:125
  145.0 0.1 collective-permute-start
  145.1 1.8 %slice.87 = f32[22,2,128,128]{3,2,1,0:T(8,128)} slice(f32[25,2,128,128]{3,2,1,0:T(8,128)S(1)} %get-tuple-element.36), slice={[0:22], [0:2], [0:128], [0:128]} | slice | bytes 5767168 | tf_op jit(solution)/shard_map/slice | solution.py:192
  146.8 5.5 %collective-permute-done = f32[129,128]{1,0:T(8,128)S(1)} collective-permute-done((f32[129,128]{1,0:T(8,128)S(1)}, f32[129,128]{1,0:T(8,128)S(1)}, u32[]{:S(2)}, u32[]{:S(2)}) %collective-permute-start) | collective-permute-done | bytes 66080 | tf_op jit(solution)/shard_map/ppermute | solution.py:191
  152.4 0.6 fusion.1
  153.0 0.0 copy-done.7
  (19 shorter events, 0.2 us)
Async XLA Ops:
  0.6 3.5 %copy-start.4 = (bf16[128,2,4,256]{3,2,1,0:T(4,128)(2,1)S(1)}, bf16[128,2,4,256]{3,2,1,0:T(4,128)(2,1)}, u32[]{:S(2)}) copy-start(bf16[128,2,4,256]{3,2,1,0:T(4,128)(2,1)} %param.11) | copy-start | bytes 1572868
  2.2 2.2 %copy-start.5 = (bf16[128,2,4,256]{3,2,1,0:T(4,128)(2,1)S(1)}, bf16[128,2,4,256]{3,2,1,0:T(4,128)(2,1)}, u32[]{:S(2)}) copy-start(bf16[128,2,4,256]{3,2,1,0:T(4,128)(2,1)} %param.12) | copy-start | bytes 1572868
  4.9 0.8 copy-start.6
  4.9 0.9 copy-start.8
  7.5 29.0 %all-to-all-start.1 = ((bf16[32,2,6528]{2,1,0:T(2,128)(2,1)}), bf16[32,2,6528]{2,1,0:T(2,128)(2,1)S(1)}, u32[]{:S(2)}, u32[]{:S(2)}) async-start(bf16[32,2,6528]{2,1,0:T(2,128)(2,1)} %all_to_all.24), calls=%async_computation.1 | async-start | bytes 1671168 | tf_op jit(solution)/shard_map/all_to_all | solution.py:180
  36.5 3.8 %copy-start.2 = (bf16[32,2,6528]{2,1,0:T(2,128)(2,1)}, bf16[32,2,6528]{2,1,0:T(2,128)(2,1)S(1)}, u32[]{:S(2)}) copy-start(bf16[32,2,6528]{2,1,0:T(2,128)(2,1)S(1)} %all-to-all-done.1) | copy-start | bytes 2506756
  36.5 25.4 %all-to-all-start = ((bf16[32,2,6528]{2,1,0:T(2,128)(2,1)}), bf16[32,2,6528]{2,1,0:T(2,128)(2,1)}, u32[]{:S(2)}, u32[]{:S(2)}) async-start(bf16[32,2,6528]{2,1,0:T(2,128)(2,1)} %all_to_all.21), calls=%async_computation | async-start | bytes 1671168 | tf_op jit(solution)/shard_map/all_to_all | solution.py:180
  42.4 23.3 %copy-start.3 = (bf16[32,2,6528]{2,1,0:T(2,128)(2,1)S(1)}, bf16[32,2,6528]{2,1,0:T(2,128)(2,1)}, u32[]{:S(2)}) copy-start(bf16[32,2,6528]{2,1,0:T(2,128)(2,1)} %copy-done.2) | copy-start | bytes 2506756
  61.9 43.4 %all-to-all-start.2 = ((bf16[32,4,6528]{2,1,0:T(4,128)(2,1)}), bf16[32,4,6528]{2,1,0:T(4,128)(2,1)}, u32[]{:S(2)}, u32[]{:S(2)}) async-start(bf16[32,4,6528]{2,1,0:T(4,128)(2,1)} %all_to_all.27), calls=%async_computation.2 | async-start | bytes 3342336 | tf_op jit(solution)/shard_map/all_to_all | solution.py:180
  68.6 0.9 copy-start
  126.1 9.4 %copy-start.1 = (bf16[64,6528]{1,0:T(8,128)(2,1)S(1)}, bf16[64,6528]{1,0:T(8,128)(2,1)}, u32[]{:S(2)}) copy-start(bf16[64,6528]{1,0:T(8,128)(2,1)} %copy-done) | copy-start | bytes 2506756
  145.0 7.4 %collective-permute-start = (f32[129,128]{1,0:T(8,128)S(1)}, f32[129,128]{1,0:T(8,128)S(1)}, u32[]{:S(2)}, u32[]{:S(2)}) collective-permute-start(f32[129,128]{1,0:T(8,128)S(1)} %pad_maximum_fusion), channel_id=1, source_target_pairs={{0,1},{1,2},{2,3},{3,4},{4,5},{5,6},{6,7},{7,8},{8,9},{9,10},{10,1... | collective-permute-start | bytes 198152 | tf_op jit(solution)/shard_map/ppermute | solution.py:191
  152.4 0.6 copy-start.7

commit v3 on v2

--- a/solution.py
+++ b/solution.py
@@ -16,7 +16,7 @@
 AXES = ("frame", "panel")
 
 
-def normal_kernel(terms, width, where_ref, rows_ref, *refs):
+def normal_kernel(terms, width, pick, where_ref, rows_ref, *refs):
     if len(refs) == 11:
         band_in, rhs_in = refs[:2]
         refs = refs[2:]
@@ -39,13 +39,18 @@
         filled = where_ref[slot]
         list_ref[count] = slot
         block_ref[count] = filled - 1
-        return count + (filled > 0).astype(jnp.int32)
+        wanted = filled > 0
+        if pick == "last":
+            wanted = filled == BLK_DEV
+        elif pick == "others":
+            wanted = wanted & (filled != BLK_DEV)
+        return count + wanted.astype(jnp.int32)
 
     count = lax.fori_loop(0, slots, gather_list, jnp.int32(0))
     list_ref[count] = 0
     block_ref[count] = TRASH
 
-    @pl.loop(0, slots // GROUP)
+    @pl.loop(0, jnp.where(count > 0, slots // GROUP, 0))
     def dense(group):
         at = pl.ds(pl.multiple_of(group * GROUP, GROUP), GROUP)
         for col in range(span // 128):
@@ -116,14 +121,14 @@
     add(last, odd_ref)
 
 
-def normal_sums(where, rows, terms, width, totals):
+def normal_sums(where, rows, terms, width, totals, pick):
     slots = rows.shape[0]
     span = terms * width
     vmem = pl.BlockSpec(memory_space=pltpu.VMEM)
     smem = pl.BlockSpec(memory_space=pltpu.SMEM)
     carried = () if totals is None else totals
     return pl.pallas_call(
-        functools.partial(normal_kernel, terms, width),
+        functools.partial(normal_kernel, terms, width, pick),
         out_shape=(
             jax.ShapeDtypeStruct((ACC_ROWS, 2, CO, CO), jnp.float32),
             jax.ShapeDtypeStruct((ACC_ROWS, 8, CO), jnp.float32),
@@ -158,7 +163,9 @@
     same_owner = owners[:, None] == owners[None, :]
     row_at = lax.broadcasted_iota(jnp.int32, (row_count, row_count), 0)
     other_at = lax.broadcasted_iota(jnp.int32, (row_count, row_count), 1)
-    position = jnp.sum((same_owner & (other_at < row_at)).astype(jnp.int32), axis=1)
+    reaches = row_offset == BLK_DEV - 1
+    ahead = jnp.where(reaches[:, None] == reaches[None, :], other_at < row_at, reaches[None, :])
+    position = jnp.sum((same_owner & ahead).astype(jnp.int32), axis=1)
     tag = jnp.broadcast_to((row_offset + 1).astype(jnp.bfloat16)[:, None], (row_count, 128))
     payload = jnp.concatenate(
         [
@@ -171,26 +178,36 @@
         axis=1,
     )
 
-    received = []
+    outgoing = []
     first = 0
     for size in waves:
         slot_at = lax.broadcasted_iota(jnp.int32, (device_count * size, row_count), 0)
         chosen = (slot_at // size == owners[None, :]) & (slot_at % size + first == position[None, :])
-        outgoing = jnp.dot(chosen.astype(jnp.bfloat16), payload, preferred_element_type=jnp.bfloat16)
-        received.append(lax.all_to_all(outgoing, AXES, split_axis=0, concat_axis=0, tiled=True))
+        outgoing.append(jnp.dot(chosen.astype(jnp.bfloat16), payload, preferred_element_type=jnp.bfloat16))
         first += size
 
+    def exchange(block):
+        return lax.all_to_all(block, AXES, split_axis=0, concat_axis=0, tiled=True)
+
+    def sums(rows, totals, pick):
+        where = rows[:, 3 * terms * width + width].astype(jnp.int32)
+        return normal_sums(where, rows, terms, width, totals, pick)
+
     totals = None
-    for rows in received:
-        where = rows[:, 3 * terms * width + width].astype(jnp.int32)
-        totals = normal_sums(where, rows, terms, width, totals)
+    rows = exchange(outgoing[0])
+    for block in outgoing[1:]:
+        rows, block = lax.optimization_barrier((rows, block))
+        coming = exchange(block)
+        totals = sums(rows, totals, "all")
+        rows = coming
+    totals = sums(rows, totals, "last")
     band, rhs = totals
-    rhs = rhs[:, 0]
-    spill = jnp.concatenate([band[BLK_DEV, 0], rhs[BLK_DEV : BLK_DEV + 1]], axis=0)
+    spill = jnp.concatenate([band[BLK_DEV, 0], rhs[BLK_DEV, 0:1]], axis=0)
     route = [(i, (i + 1) % device_count) for i in range(device_count)]
     spill = lax.ppermute(spill, AXES, route)
+    band, rhs = sums(rows, totals, "others")
     normal_band = band[:BLK_DEV].at[0, 0].add(spill[:CO])
-    normal_rhs = rhs[:BLK_DEV].at[0].add(spill[CO])
+    normal_rhs = rhs[:BLK_DEV, 0].at[0].add(spill[CO])
     return (normal_band, normal_rhs)
 
 

time: 154 us -> 144 us (0.935)
  waiting for transfers between devices: 80.9 us -> 58.6 us
  local copies, waits for them, and re-layouts: 14 us -> 21.6 us
  matrix products: 1.61 us -> 3.43 us
    all_to_all x3, waiting for transfers between devices: 75.3 us -> 58.6 us  [exchange(): return lax.all_to_all(block, AXES, split_axis=0, concat_axis=0, tiled=True)]
    ppermute x1, waiting for transfers between devices: 5.53 us -> 0.01 us  [on_device(): spill = lax.ppermute(spill, AXES, route)]
    unnamed x23 -> x25, local copies, waits for them, and re-layouts: 1.74 us -> 5.6 us
    all_to_all x6, local copies, waits for them, and re-layouts: 9.26 us -> 13 us  [exchange(): return lax.all_to_all(block, AXES, split_axis=0, concat_axis=0, tiled=True)]
    dot_general x3, matrix products: 1.61 us -> 3.43 us  [on_device(): jnp.dot(chosen.astype(jnp.bfloat16), payload, preferred_element_type=jnp....]
    pallas_call x3 -> x4, Pallas kernels: 36.7 us -> 38 us  [normal_sums(): pl.pallas_call(functools.partial(normal_kernel, terms, width, pick), out_...]
  transfers between devices with their start and end apart: 4 -> 4, of which waited for: 4 -> 2; matrix products, arithmetic and copies ran while one was open for 2% -> 3% of each run, Pallas kernels for 0% -> 26%
where the time goes in v3:
time: 144 us; the launch traced here: 142 us
  waiting for transfers between devices  58.6 us (41%)
  Pallas kernels  38 us (26%)
  local copies, waits for them, and re-layouts  21.6 us (15%)
  starting transfers between devices  15.4 us (11%)
  other arithmetic  4.02 us (3%)
  matrix products  3.43 us (2%)
    all_to_all x3, waiting for transfers between devices, exchange(): return lax.all_to_all(block, AXES, split_axis=0, concat_axis=0, tiled=True)  58.6 us
    pallas_call x4, Pallas kernels, normal_sums(): pl.pallas_call(functools.partial(normal_kernel, terms, width, pick), out_...  38 us
    all_to_all x3, starting transfers between devices, exchange(): return lax.all_to_all(block, AXES, split_axis=0, concat_axis=0, tiled=True)  15.2 us
    all_to_all x6, local copies, waits for them, and re-layouts, exchange(): return lax.all_to_all(block, AXES, split_axis=0, concat_axis=0, tiled=True)  13 us
    unnamed x25, local copies, waits for them, and re-layouts  5.6 us
    dot_general x3, matrix products, on_device(): jnp.dot(chosen.astype(jnp.bfloat16), payload, preferred_element_type=jnp....  3.43 us
  transfers between devices with their start and end apart: 4, of which 2 were waited for; matrix products, arithmetic and copies ran while one was open for 3% of the time, Pallas kernels for 26%

profile of v3, /device:TPU:0, one launch (start us, length us, event | category | flops | bytes accessed | tf_op | source)
XLA Modules:
  0.0 142.1 jit_solution(1769113793911389520)
XLA Ops:
  0.6 0.0 copy-start.5
  0.6 0.7 add_convert_fusion
  1.4 0.7 broadcast_compare_fusion
  2.0 0.0 copy-start.6
  2.1 1.5 %convert_element_type.29 = bf16[128,2,4,256]{3,2,1,0:T(4,128)(2,1)S(1)} convert(s32[128,2,4,256]{3,2,1,0:T(4,128)} %param.10) | non-fusion elementwise | flops 262144 | bytes 1572864 | tf_op jit(solution)/shard_map/convert_element_type | solution.py:172
  3.5 0.4 reshape.96
  3.9 0.0 copy-done.5
  3.9 0.0 copy-start.8
  3.9 0.4 reshape.97
  4.3 0.0 copy-done.6
  4.3 0.4 reshape.98
  4.7 0.0 copy-start.7
  4.8 0.0 copy-done.8
  4.8 0.2 convert_reduce_fusion.1
  5.0 0.5 copy-done.7
  5.5 0.1 broadcast_dynamic-update-slice_fusion
  5.6 0.7 fusion.3
  6.4 1.4 all_to_all.23
  7.7 7.4 %all-to-all-start = ((bf16[32,4,6528]{2,1,0:T(4,128)(2,1)}), bf16[32,4,6528]{2,1,0:T(4,128)(2,1)}, u32[]{:S(2)}, u32[]{:S(2)}) async-start(bf16[32,4,6528]{2,1,0:T(4,128)(2,1)} %all_to_all.23), calls=%async_computation | async-start | bytes 3342336 | tf_op jit(solution)/shard_map/all_to_all | solution.py:190
  15.2 1.4 fusion.21
  16.6 38.3 %all-to-all-done = bf16[32,4,6528]{2,1,0:T(4,128)(2,1)} async-done(((bf16[32,4,6528]{2,1,0:T(4,128)(2,1)}), bf16[32,4,6528]{2,1,0:T(4,128)(2,1)}, u32[]{:S(2)}, u32[]{:S(2)}) %all-to-all-start) | async-done | bytes 1671200 | tf_op jit(solution)/shard_map/all_to_all | solution.py:190
  54.9 2.7 %all_to_all.25.rows_ref = bf16[128,6528]{1,0:T(8,128)(2,1)S(1)} reshape(bf16[32,4,6528]{2,1,0:T(4,128)(2,1)} %all-to-all-done) | data formatting | bytes 3342336 | tf_op jit(solution)/shard_map/all_to_all | solution.py:190
  57.6 2.9 %all_to_all.26 = bf16[32,2,6528]{2,1,0:T(2,128)(2,1)} reshape(bf16[64,6528]{1,0:T(8,128)(2,1)} %fusion.21) | data formatting | bytes 1671168 | tf_op jit(solution)/shard_map/all_to_all | solution.py:190
  60.5 4.1 %all-to-all-start.1 = ((bf16[32,2,6528]{2,1,0:T(2,128)(2,1)}), bf16[32,2,6528]{2,1,0:T(2,128)(2,1)}, u32[]{:S(2)}, u32[]{:S(2)}) async-start(bf16[32,2,6528]{2,1,0:T(2,128)(2,1)} %all_to_all.26), calls=%async_computation.1 | async-start | bytes 1671168 | tf_op jit(solution)/shard_map/all_to_all | solution.py:190
  64.6 1.3 fusion.19
  66.0 20.3 %all-to-all-done.1 = bf16[32,2,6528]{2,1,0:T(2,128)(2,1)} async-done(((bf16[32,2,6528]{2,1,0:T(2,128)(2,1)}), bf16[32,2,6528]{2,1,0:T(2,128)(2,1)}, u32[]{:S(2)}, u32[]{:S(2)}) %all-to-all-start.1) | async-done | bytes 835616 | tf_op jit(solution)/shard_map/all_to_all | solution.py:190
  86.3 2.4 %all_to_all.28.rows_ref = bf16[64,6528]{1,0:T(8,128)(2,1)S(1)} reshape(bf16[32,2,6528]{2,1,0:T(2,128)(2,1)} %all-to-all-done.1) | data formatting | bytes 1671168 | tf_op jit(solution)/shard_map/all_to_all | solution.py:190
  88.7 0.0 copy-done.4
  88.7 1.2 all_to_all.29
  89.9 3.7 %all-to-all-start.2 = ((bf16[32,2,6528]{2,1,0:T(2,128)(2,1)}), bf16[32,2,6528]{2,1,0:T(2,128)(2,1)}, u32[]{:S(2)}, u32[]{:S(2)}) async-start(bf16[32,2,6528]{2,1,0:T(2,128)(2,1)} %all_to_all.29), calls=%async_computation.2 | async-start | bytes 1671168 | tf_op jit(solution)/shard_map/all_to_all | solution.py:190
  93.6 0.1 convert_reduce_fusion.where_ref
  93.7 17.8 %shard_map.77 = (f32[25,2,128,128]{3,2,1,0:T(8,128)S(1)}, f32[25,8,128]{2,1,0:T(8,128)S(1)}) custom-call(s32[128]{0:T(128)S(1)} %convert_reduce_fusion.where_ref, bf16[128,6528]{1,0:T(8,128)(2,1)S(1)} %all_to_all.25.rows_ref), custom_call_target="tpu_custom_call" | custom-call | flops 2560000000 | bytes 10000000 | tf_op jit(solution)/shard_map/pallas_call | solution.py:130
  111.5 0.1 convert_reduce_fusion.2.where_ref
  111.6 9.4 %shard_map.78 = (f32[25,2,128,128]{3,2,1,0:T(8,128)S(1)}, f32[25,8,128]{2,1,0:T(8,128)S(1)}) custom-call(s32[64]{0:T(128)S(1)} %convert_reduce_fusion.2.where_ref, bf16[64,6528]{1,0:T(8,128)(2,1)S(1)} %all_to_all.28.rows_ref, f32[25,2,128,128]{3,2,1,0:T(8,128)S(1)} %get-tuple-element.42.refs_0_, f32[25,8,128]{2,1,0:T(8,128)S(1)} %get-tuple-element.43.refs_1_), custom_call_target="tpu_custom_call" | custom-call | flops 1280000000 | bytes 10000000 | tf_op jit(solution)/shard_map/pallas_call | solution.py:130
  121.0 0.0 copy-start.2
  121.0 1.7 %copy-done.2 = f32[25,2,128,128]{3,2,1,0:T(8,128)} copy-done((f32[25,2,128,128]{3,2,1,0:T(8,128)}, f32[25,2,128,128]{3,2,1,0:T(8,128)S(1)}, u32[]{:S(2)}) %copy-start.2) | copy-done | bytes 3276824
  122.7 0.0 all-to-all-done.2
  122.7 2.4 %all_to_all.31.rows_ref = bf16[64,6528]{1,0:T(8,128)(2,1)S(1)} reshape(bf16[32,2,6528]{2,1,0:T(2,128)(2,1)} %all-to-all-done.2) | data formatting | bytes 1671168 | tf_op jit(solution)/shard_map/all_to_all | solution.py:190
  125.1 0.0 copy-start
  125.1 0.1 convert_reduce_fusion.3.where_ref
  125.2 2.1 %copy-done.3 = f32[25,2,128,128]{3,2,1,0:T(8,128)S(1)} copy-done((f32[25,2,128,128]{3,2,1,0:T(8,128)S(1)}, f32[25,2,128,128]{3,2,1,0:T(8,128)}, u32[]{:S(2)}) %copy-start.3) | copy-done | bytes 3276824
  127.3 1.5 %shard_map.79 = (f32[25,2,128,128]{3,2,1,0:T(8,128)S(1)}, f32[25,8,128]{2,1,0:T(8,128)S(1)}) custom-call(s32[64]{0:T(128)S(1)} %convert_reduce_fusion.3.where_ref, bf16[64,6528]{1,0:T(8,128)(2,1)S(1)} %all_to_all.31.rows_ref, f32[25,2,128,128]{3,2,1,0:T(8,128)S(1)} %copy-done.3, f32[25,8,128]{2,1,0:T(8,128)S(1)} %get-tuple-element.45.refs_1_), custom_call_target="tpu_custom_call" | custom-call | flops 1280000000 | bytes 10000000 | tf_op jit(solution)/shard_map/pallas_call | solution.py:130
  128.8 0.2 collective-permute-start
  129.1 1.1 copy-done.1
  130.2 9.4 %shard_map.80 = (f32[25,2,128,128]{3,2,1,0:T(8,128)S(1)}, f32[25,8,128]{2,1,0:T(8,128)S(1)}) custom-call(s32[64]{0:T(128)S(1)} %convert_reduce_fusion.3.where_ref, bf16[64,6528]{1,0:T(8,128)(2,1)S(1)} %copy-done.1, f32[25,2,128,128]{3,2,1,0:T(8,128)S(1)} %get-tuple-element.46.refs_0_, f32[25,8,128]{2,1,0:T(8,128)S(1)} %get-tuple-element.47.refs_1_), custom_call_target="tpu_custom_call" | custom-call | flops 1280000000 | bytes 10000000 | tf_op jit(solution)/shard_map/pallas_call | solution.py:130
  139.7 1.8 %slice.79 = f32[22,2,128,128]{3,2,1,0:T(8,128)} slice(f32[25,2,128,128]{3,2,1,0:T(8,128)S(1)} %get-tuple-element.48), slice={[0:22], [0:2], [0:128], [0:128]} | slice | bytes 5767168 | tf_op jit(solution)/shard_map/slice | solution.py:209
  141.4 0.0 collective-permute-done
  141.5 0.6 fusion.1
  (23 shorter events, 0.2 us)
Async XLA Ops:
  0.6 3.3 %copy-start.5 = (bf16[128,2,4,256]{3,2,1,0:T(4,128)(2,1)S(1)}, bf16[128,2,4,256]{3,2,1,0:T(4,128)(2,1)}, u32[]{:S(2)}) copy-start(bf16[128,2,4,256]{3,2,1,0:T(4,128)(2,1)} %param.11) | copy-start | bytes 1572868
  2.0 2.3 %copy-start.6 = (bf16[128,2,4,256]{3,2,1,0:T(4,128)(2,1)S(1)}, bf16[128,2,4,256]{3,2,1,0:T(4,128)(2,1)}, u32[]{:S(2)}) copy-start(bf16[128,2,4,256]{3,2,1,0:T(4,128)(2,1)} %param.12) | copy-start | bytes 1572868
  3.9 0.8 copy-start.8
  4.7 0.8 copy-start.7
  7.7 47.1 %all-to-all-start = ((bf16[32,4,6528]{2,1,0:T(4,128)(2,1)}), bf16[32,4,6528]{2,1,0:T(4,128)(2,1)}, u32[]{:S(2)}, u32[]{:S(2)}) async-start(bf16[32,4,6528]{2,1,0:T(4,128)(2,1)} %all_to_all.23), calls=%async_computation | async-start | bytes 3342336 | tf_op jit(solution)/shard_map/all_to_all | solution.py:190
  60.5 25.7 %all-to-all-start.1 = ((bf16[32,2,6528]{2,1,0:T(2,128)(2,1)}), bf16[32,2,6528]{2,1,0:T(2,128)(2,1)}, u32[]{:S(2)}, u32[]{:S(2)}) async-start(bf16[32,2,6528]{2,1,0:T(2,128)(2,1)} %all_to_all.26), calls=%async_computation.1 | async-start | bytes 1671168 | tf_op jit(solution)/shard_map/all_to_all | solution.py:190
  66.0 22.7 %copy-start.4 = (bf16[64,6528]{1,0:T(8,128)(2,1)S(1)}, bf16[64,6528]{1,0:T(8,128)(2,1)}, u32[]{:S(2)}) copy-start(bf16[64,6528]{1,0:T(8,128)(2,1)} %fusion.19) | copy-start | bytes 2506756
  89.9 32.8 %all-to-all-start.2 = ((bf16[32,2,6528]{2,1,0:T(2,128)(2,1)}), bf16[32,2,6528]{2,1,0:T(2,128)(2,1)}, u32[]{:S(2)}, u32[]{:S(2)}) async-start(bf16[32,2,6528]{2,1,0:T(2,128)(2,1)} %all_to_all.29), calls=%async_computation.2 | async-start | bytes 1671168 | tf_op jit(solution)/shard_map/all_to_all | solution.py:190
  121.0 1.7 %copy-start.2 = (f32[25,2,128,128]{3,2,1,0:T(8,128)}, f32[25,2,128,128]{3,2,1,0:T(8,128)S(1)}, u32[]{:S(2)}) copy-start(f32[25,2,128,128]{3,2,1,0:T(8,128)S(1)} %get-tuple-element.44.refs_0_) | copy-start | bytes 9830404
  125.1 3.7 %copy-start = (bf16[64,6528]{1,0:T(8,128)(2,1)}, bf16[64,6528]{1,0:T(8,128)(2,1)S(1)}, u32[]{:S(2)}) copy-start(bf16[64,6528]{1,0:T(8,128)(2,1)S(1)} %all_to_all.31.rows_ref) | copy-start | bytes 2506756
  125.2 2.1 %copy-start.3 = (f32[25,2,128,128]{3,2,1,0:T(8,128)S(1)}, f32[25,2,128,128]{3,2,1,0:T(8,128)}, u32[]{:S(2)}) copy-start(f32[25,2,128,128]{3,2,1,0:T(8,128)} %copy-done.2) | copy-start | bytes 9830404
  128.8 12.6 %collective-permute-start = (f32[129,128]{1,0:T(8,128)S(1)}, f32[129,128]{1,0:T(8,128)S(1)}, u32[]{:S(2)}, u32[]{:S(2)}) collective-permute-start(f32[129,128]{1,0:T(8,128)S(1)} %pad_maximum_fusion), channel_id=1, source_target_pairs={{0,1},{1,2},{2,3},{3,4},{4,5},{5,6},{6,7},{7,8},{8,9},{9,10},{10,1... | collective-permute-start | bytes 198152 | tf_op jit(solution)/shard_map/ppermute | solution.py:207
  129.1 1.1 copy-start.1
  141.5 0.7 copy-start.9

commit v4 on v3

--- a/solution.py
+++ b/solution.py
@@ -16,17 +16,17 @@
 AXES = ("frame", "panel")
 
 
-def normal_kernel(terms, width, pick, where_ref, rows_ref, *refs):
+def normal_kernel(neighbors, width, pick, where_ref, rows_ref, *refs):
     if len(refs) == 11:
         band_in, rhs_in = refs[:2]
         refs = refs[2:]
     else:
         band_in = rhs_in = None
     band_ref, rhs_ref, index_ref, weight_ref, force_ref, even_ref, odd_ref, list_ref, block_ref = refs
-    slots = rows_ref.shape[0]
-    span = terms * width
+    slots = where_ref.shape[0]
     lanes = width // 128
-    neighbors = terms // 2
+    pieces = rows_ref.shape[0] // slots
+    span = neighbors * 128
 
     if band_in is None:
         band_ref[...] = jnp.zeros_like(band_ref)
@@ -50,7 +50,7 @@
     list_ref[count] = 0
     block_ref[count] = TRASH
 
-    @pl.loop(0, jnp.where(count > 0, slots // GROUP, 0))
+    @pl.loop(0, jnp.where(count > 0, slots * pieces // GROUP, 0))
     def dense(group):
         at = pl.ds(pl.multiple_of(group * GROUP, GROUP), GROUP)
         for col in range(span // 128):
@@ -64,21 +64,20 @@
             weight_ref[1, col, at, :] = p * (3.0 * cube - 6.0 * square + 4.0)
             weight_ref[2, col, at, :] = p * (3.0 * (square - cube + t) + 1.0)
             weight_ref[3, col, at, :] = p * cube
+        force_ref[at, :] = rows_ref[at, pl.ds(3 * span, 128)].astype(jnp.float32)
+
+    sub = lax.broadcasted_iota(jnp.int32, (8, 128), 0)
+
+    def build(slot, design_ref):
+        base = slot * pieces
         for lane in range(lanes):
-            force_ref[lane, at, :] = rows_ref[at, pl.ds(3 * span + lane * 128, 128)].astype(jnp.float32)
-
-    sub = lax.broadcasted_iota(jnp.int32, (8, 128), 0)
-
-    def build(slot, design_ref):
-        at = pl.ds(slot, 1)
-        for lane in range(lanes):
-            force = jnp.broadcast_to(force_ref[lane, at, :], (HEAD, 128)).astype(jnp.bfloat16)
+            force = jnp.broadcast_to(force_ref[pl.ds(base + lane, 1), :], (HEAD, 128)).astype(jnp.bfloat16)
             design_ref[0:HEAD, lane * 128 : lane * 128 + 128] = force
         for s in range(2):
             for lane in range(lanes):
+                at = pl.ds(base + s * lanes + lane, 1)
                 tiles = [None] * (CO // 8)
-                for n in range(neighbors):
-                    col = (s * neighbors + n) * lanes + lane
+                for col in range(neighbors):
                     index = jnp.broadcast_to(index_ref[col, at, :], (8, 128))
                     m = (sub - index) & 7
                     value = jnp.where(m == 3, jnp.broadcast_to(weight_ref[3, col, at, :], (8, 128)), 0.0)
@@ -121,14 +120,14 @@
     add(last, odd_ref)
 
 
-def normal_sums(where, rows, terms, width, totals, pick):
-    slots = rows.shape[0]
-    span = terms * width
+def normal_sums(where, rows, neighbors, width, totals, pick):
+    slots = where.shape[0]
+    held = rows.shape[0]
     vmem = pl.BlockSpec(memory_space=pltpu.VMEM)
     smem = pl.BlockSpec(memory_space=pltpu.SMEM)
     carried = () if totals is None else totals
     return pl.pallas_call(
-        functools.partial(normal_kernel, terms, width, pick),
+        functools.partial(normal_kernel, neighbors, width, pick),
         out_shape=(
             jax.ShapeDtypeStruct((ACC_ROWS, 2, CO, CO), jnp.float32),
             jax.ShapeDtypeStruct((ACC_ROWS, 8, CO), jnp.float32),
@@ -136,9 +135,9 @@
         in_specs=[smem, vmem] + [vmem] * len(carried),
         out_specs=(vmem, vmem),
         scratch_shapes=[
-            pltpu.VMEM((span // 128, slots, 128), jnp.int32),
-            pltpu.VMEM((4, span // 128, slots, 128), jnp.float32),
-            pltpu.VMEM((width // 128, slots, 128), jnp.float32),
+            pltpu.VMEM((neighbors, held, 128), jnp.int32),
+            pltpu.VMEM((4, neighbors, held, 128), jnp.float32),
+            pltpu.VMEM((held, 128), jnp.float32),
             pltpu.VMEM((HEAD + 2 * CO, width), jnp.bfloat16),
             pltpu.VMEM((HEAD + 2 * CO, width), jnp.bfloat16),
             pltpu.SMEM((slots + 8,), jnp.int32),
@@ -151,47 +150,99 @@
     )(where, rows, *carried)
 
 
+def send_kernel(parts, waves, *refs):
+    index_ref, frac_ref, proj_ref, force_ref, owner_col, offset_col, owner_row, offset_row = refs[:8]
+    out_refs, payload_ref = refs[8:-1], refs[-1]
+    slot_width, neighbors, lanes = parts
+    pieces = slot_width * lanes
+    count = index_ref.shape[0]
+    for s in range(slot_width):
+        for lane in range(lanes):
+            piece = s * lanes + lane
+            at = slice(piece * count, (piece + 1) * count)
+            for kind, ref in enumerate((index_ref, frac_ref, proj_ref)):
+                for n in range(neighbors):
+                    source = ((s * neighbors + n) * lanes + lane) * 128
+                    column = (kind * neighbors + n) * 128
+                    payload_ref[at, column : column + 128] = ref[:, source : source + 128]
+            column = 3 * neighbors * 128
+            if s == 0:
+                payload_ref[at, column : column + 128] = force_ref[:, lane * 128 : lane * 128 + 128]
+            else:
+                tag = jnp.broadcast_to((offset_col[...] + 1).astype(jnp.float32), (count, 128))
+                payload_ref[at, column : column + 128] = tag.astype(jnp.bfloat16)
+
+    shape = (count, count)
+    other_at = lax.broadcasted_iota(jnp.int32, shape, 0)
+    row_at = lax.broadcasted_iota(jnp.int32, shape, 1)
+    other_key = jnp.where(offset_col[...] == BLK_DEV - 1, 0, count) + other_at
+    row_key = jnp.where(offset_row[...] == BLK_DEV - 1, 0, count) + row_at
+    before = (owner_col[...] == owner_row[...]) & (other_key < row_key)
+    position = jnp.sum(jnp.where(before, 1.0, 0.0), axis=0, keepdims=True).astype(jnp.int32)
+
+    first = 0
+    for size, out_ref in zip(waves, out_refs):
+        inside = (position >= first) & (position < first + size)
+        start = owner_row[...] * (size * pieces) + (position - first) * pieces
+        target = jnp.concatenate([jnp.where(inside, start + piece, -1) for piece in range(pieces)], axis=1)
+
+        @pl.loop(0, out_ref.shape[0] // 128)
+        def place(tile):
+            at = pl.multiple_of(tile * 128, 128)
+            row_id = lax.broadcasted_iota(jnp.int32, (128, pieces * count), 0) + at
+            chosen = jnp.where(row_id == target, 1.0, 0.0).astype(jnp.bfloat16)
+            moved = jnp.dot(chosen, payload_ref[...], preferred_element_type=jnp.float32)
+            out_ref[pl.ds(at, 128), :] = moved.astype(jnp.bfloat16)
+
+        first += size
+
+
+def send_blocks(index, frac, proj, forces, owner_col, offset_col, owner_row, offset_row, parts, waves, device_count):
+    slot_width, neighbors, lanes = parts
+    pieces = slot_width * lanes
+    width = (3 * neighbors + 1) * 128
+    vmem = pl.BlockSpec(memory_space=pltpu.VMEM)
+    return pl.pallas_call(
+        functools.partial(send_kernel, parts, waves),
+        out_shape=[jax.ShapeDtypeStruct((device_count * size * pieces, width), jnp.bfloat16) for size in waves],
+        in_specs=[vmem] * 8,
+        out_specs=[vmem] * len(waves),
+        scratch_shapes=[pltpu.VMEM((pieces * index.shape[0], width), jnp.bfloat16)],
+        compiler_params=pltpu.CompilerParams(vmem_limit_bytes=40 * 1024 * 1024),
+    )(index, frac, proj, forces, owner_col, offset_col, owner_row, offset_row)
+
+
 def on_device(spline_index, spline_frac, projection, forces, row_owner, row_offset):
     row_count, slot_width, neighbors, design_rows = spline_index.shape
-    terms = slot_width * neighbors
+    lanes = design_rows // 128
+    pieces = slot_width * lanes
     device_count = lax.axis_size(AXES)
     capacity = max(2, 2 * row_count // device_count)
     width = design_rows
-    waves = [size for size in (capacity // 2, capacity // 4, capacity - capacity // 2 - capacity // 4) if size]
-
-    owners = row_owner[:, 0]
-    same_owner = owners[:, None] == owners[None, :]
-    row_at = lax.broadcasted_iota(jnp.int32, (row_count, row_count), 0)
-    other_at = lax.broadcasted_iota(jnp.int32, (row_count, row_count), 1)
-    reaches = row_offset == BLK_DEV - 1
-    ahead = jnp.where(reaches[:, None] == reaches[None, :], other_at < row_at, reaches[None, :])
-    position = jnp.sum((same_owner & ahead).astype(jnp.int32), axis=1)
-    tag = jnp.broadcast_to((row_offset + 1).astype(jnp.bfloat16)[:, None], (row_count, 128))
-    payload = jnp.concatenate(
-        [
-            spline_index.astype(jnp.bfloat16).reshape(row_count, terms * width),
-            spline_frac.reshape(row_count, terms * width),
-            projection.reshape(row_count, terms * width),
-            forces,
-            tag,
-        ],
-        axis=1,
+    late = max(1, capacity // 4)
+    waves = [capacity - late, late]
+
+    flat = (row_count, slot_width * neighbors * design_rows)
+    outgoing = send_blocks(
+        spline_index.astype(jnp.bfloat16).reshape(flat),
+        spline_frac.reshape(flat),
+        projection.reshape(flat),
+        forces,
+        row_owner,
+        row_offset[:, None],
+        row_owner.reshape(1, row_count),
+        row_offset[None, :],
+        (slot_width, neighbors, lanes),
+        waves,
+        device_count,
     )
-
-    outgoing = []
-    first = 0
-    for size in waves:
-        slot_at = lax.broadcasted_iota(jnp.int32, (device_count * size, row_count), 0)
-        chosen = (slot_at // size == owners[None, :]) & (slot_at % size + first == position[None, :])
-        outgoing.append(jnp.dot(chosen.astype(jnp.bfloat16), payload, preferred_element_type=jnp.bfloat16))
-        first += size
 
     def exchange(block):
         return lax.all_to_all(block, AXES, split_axis=0, concat_axis=0, tiled=True)
 
     def sums(rows, totals, pick):
-        where = rows[:, 3 * terms * width + width].astype(jnp.int32)
-        return normal_sums(where, rows, terms, width, totals, pick)
+        where = rows[:, 3 * neighbors * 128].reshape(-1, pieces)[:, pieces - 1].astype(jnp.int32)
+        return normal_sums(where, rows, neighbors, width, totals, pick)
 
     totals = None
     rows = exchange(outgoing[0])

time: 144 us -> 125 us (0.87)
  blocking collectives: 0 us -> 66.4 us
  waiting for transfers between devices: 58.6 us -> 0.01 us
  starting transfers between devices: 15.4 us -> 3.19 us
  local copies, waits for them, and re-layouts: 21.6 us -> 9.88 us
  matrix products: 3.43 us -> 0 us
  Pallas kernels: 38 us -> 40.9 us
  other arithmetic: 4.02 us -> 2.43 us
    all_to_all x0 -> x1, blocking collectives: none -> 66.4 us  [exchange(): return lax.all_to_all(block, AXES, split_axis=0, concat_axis=0, tiled=True)]
    all_to_all x3 -> x1, waiting for transfers between devices: 58.6 us -> 0.01 us  [exchange(): return lax.all_to_all(block, AXES, split_axis=0, concat_axis=0, tiled=True)]
    all_to_all x6 -> x0, local copies, waits for them, and re-layouts: 13 us -> none  [exchange(): return lax.all_to_all(block, AXES, split_axis=0, concat_axis=0, tiled=True)]
    all_to_all x3 -> x1, starting transfers between devices: 15.2 us -> 2.9 us  [exchange(): return lax.all_to_all(block, AXES, split_axis=0, concat_axis=0, tiled=True)]
    dot_general x3 -> x0, matrix products: 3.43 us -> none  [on_device(): jnp.dot(chosen.astype(jnp.bfloat16), payload, preferred_element_type=jnp....]
    pallas_call x4, Pallas kernels: 38 us -> 40.9 us  [the longest x3 37.3 us: normal_sums(): pl.pallas_call(functools.partial(normal_kernel, neighbors, width, pick),...]
    unnamed x25 -> x24, local copies, waits for them, and re-layouts: 5.6 us -> 5.55 us
  transfers between devices with their start and end apart: 4 -> 2, of which waited for: 2 -> 0; matrix products, arithmetic and copies ran while one was open for 3% -> 2% of each run, Pallas kernels for 26% -> 29%
where the time goes in v4:
time: 125 us; the launch traced here: 124 us
  blocking collectives  66.4 us (53%)
  Pallas kernels  40.9 us (33%)
  local copies, waits for them, and re-layouts  9.88 us (8%)
  starting transfers between devices  3.19 us (3%)
  other arithmetic  2.43 us (2%)
    all_to_all x1, blocking collectives, exchange(): return lax.all_to_all(block, AXES, split_axis=0, concat_axis=0, tiled=True)  66.4 us
    pallas_call x3, Pallas kernels, normal_sums(): pl.pallas_call(functools.partial(normal_kernel, neighbors, width, pick),...  37.3 us
    unnamed x24, local copies, waits for them, and re-layouts  5.55 us
    pallas_call x1, Pallas kernels, send_blocks(): pl.pallas_call(functools.partial(send_kernel, parts, waves), out_shape=[j...  3.64 us
    all_to_all x1, starting transfers between devices, exchange(): return lax.all_to_all(block, AXES, split_axis=0, concat_axis=0, tiled=True)  2.9 us
  transfers between devices with their start and end apart: 2, of which 0 were waited for; matrix products, arithmetic and copies ran while one was open for 2% of the time, Pallas kernels for 29%

profile of v4, /device:TPU:0, one launch (start us, length us, event | category | flops | bytes accessed | tf_op | source)
XLA Modules:
  0.0 123.7 jit_solution(17809948080697083694)
XLA Ops:
  0.6 0.0 copy-start.5
  0.6 0.0 copy-start.4
  0.7 0.0 copy-start.8
  0.7 0.0 copy-start.9
  0.7 0.0 copy-start.3
  0.7 0.9 copy.14.refs_5_
  1.5 0.8 copy.13.refs_4_
  2.3 1.4 %convert_element_type.14 = bf16[128,2,4,256]{3,2,1,0:T(4,128)(2,1)S(1)} convert(s32[128,2,4,256]{3,2,1,0:T(4,128)} %param.10) | non-fusion elementwise | flops 262144 | bytes 1572864 | tf_op jit(solution)/shard_map/convert_element_type | solution.py:227
  3.7 0.4 reshape.90.refs_0_
  4.1 0.0 copy-done.8
  4.1 0.4 reshape.91.refs_1_
  4.5 0.0 copy-done.9
  4.5 0.4 reshape.92.refs_2_
  4.9 0.0 copy-done.5
  4.9 0.0 copy-done.4
  4.9 0.0 copy-done.3
  4.9 3.6 %shard_map.77 = (bf16[768,1664]{1,0:T(8,128)(2,1)S(1)}, bf16[256,1664]{1,0:T(8,128)(2,1)S(1)}) custom-call(bf16[128,2048]{1,0:T(8,128)(2,1)S(1)} %reshape.90.refs_0_, bf16[128,2048]{1,0:T(8,128)(2,1)S(1)} %reshape.91.refs_1_, bf16[128,2048]{1,0:T(8,128)(2,1)S(1)} %reshape.92.refs_2_, bf16[128,256]{1,0:T(8,128)(2,1)S(1)} %copy-done.3, ...), custom_call_target="tpu_custom_call" | custom-call | tf_op jit(solution)/shard_map/pallas_call | solution.py:205
  8.5 0.0 copy-start.2
  8.6 66.4 %all_to_all.23 = bf16[32,24,1664]{2,1,0:T(8,128)(2,1)S(1)} all-to-all(bf16[32,24,1664]{2,1,0:T(8,128)(2,1)S(1)} %bitcast.24), channel_id=1, replica_groups=mesh['frame'=4,'panel'=8] {'frame','panel'}, dimensions={0} | all-to-all | bytes 5111808 | tf_op jit(solution)/shard_map/all_to_all | solution.py:241
  75.0 0.0 copy-done.2
  75.0 2.9 %all-to-all-start.1 = ((bf16[32,8,1664]{2,1,0:T(8,128)(2,1)}), bf16[32,8,1664]{2,1,0:T(8,128)(2,1)S(1)}, u32[]{:S(2)}, u32[]{:S(2)}) async-start(bf16[32,8,1664]{2,1,0:T(8,128)(2,1)} %bitcast.28), calls=%async_computation.1 | async-start | bytes 1703936 | tf_op jit(solution)/shard_map/all_to_all | solution.py:241
  77.9 0.1 slice_reduce_fusion
  78.0 0.1 reshape_squeeze.8
  78.2 0.2 convert_reduce_fusion.where_ref
  78.4 26.4 %shard_map.78 = (f32[25,2,128,128]{3,2,1,0:T(8,128)S(1)}, f32[25,8,128]{2,1,0:T(8,128)S(1)}) custom-call(s32[192]{0:T(256)S(1)} %convert_reduce_fusion.where_ref, bf16[768,1664]{1,0:T(8,128)(2,1)S(1)} %bitcast.23), custom_call_target="tpu_custom_call" | custom-call | flops 3840000000 | bytes 10000000 | tf_op jit(solution)/shard_map/pallas_call | solution.py:129
  104.7 0.0 copy-start.6
  104.7 1.7 %copy-done.6 = f32[25,2,128,128]{3,2,1,0:T(8,128)} copy-done((f32[25,2,128,128]{3,2,1,0:T(8,128)}, f32[25,2,128,128]{3,2,1,0:T(8,128)S(1)}, u32[]{:S(2)}) %copy-start.6) | copy-done | bytes 3276824
  106.4 0.0 all-to-all-done.1
  106.4 0.0 copy-start
  106.4 0.1 slice_reduce_fusion.1
  106.5 0.1 reshape_squeeze.7
  106.7 0.2 convert_reduce_fusion.1.where_ref
  106.8 0.0 copy-start.7
  106.8 1.9 %copy-done.7 = f32[25,2,128,128]{3,2,1,0:T(8,128)S(1)} copy-done((f32[25,2,128,128]{3,2,1,0:T(8,128)S(1)}, f32[25,2,128,128]{3,2,1,0:T(8,128)}, u32[]{:S(2)}) %copy-start.7) | copy-done | bytes 3276824
  108.8 1.5 %shard_map.79 = (f32[25,2,128,128]{3,2,1,0:T(8,128)S(1)}, f32[25,8,128]{2,1,0:T(8,128)S(1)}) custom-call(s32[64]{0:T(128)S(1)} %convert_reduce_fusion.1.where_ref, bf16[256,1664]{1,0:T(8,128)(2,1)S(1)} %bitcast.26, f32[25,2,128,128]{3,2,1,0:T(8,128)S(1)} %copy-done.7, f32[25,8,128]{2,1,0:T(8,128)S(1)} %get-tuple-element.41.refs_1_), custom_call_target="tpu_custom_call" | custom-call | flops 1280000000 | bytes 10000000 | tf_op jit(solution)/shard_map/pallas_call | solution.py:129
  110.3 0.0 copy-done
  110.3 0.3 collective-permute-start
  110.6 0.0 copy-start.1
  110.6 1.2 copy-done.1
  111.7 9.4 %shard_map.80 = (f32[25,2,128,128]{3,2,1,0:T(8,128)S(1)}, f32[25,8,128]{2,1,0:T(8,128)S(1)}) custom-call(s32[64]{0:T(128)S(1)} %convert_reduce_fusion.1.where_ref, bf16[256,1664]{1,0:T(8,128)(2,1)S(1)} %bitcast.27, f32[25,2,128,128]{3,2,1,0:T(8,128)S(1)} %get-tuple-element.42.refs_0_, f32[25,8,128]{2,1,0:T(8,128)S(1)} %get-tuple-element.43.refs_1_), custom_call_target="tpu_custom_call" | custom-call | flops 1280000000 | bytes 10000000 | tf_op jit(solution)/shard_map/pallas_call | solution.py:129
  121.2 1.8 %slice.84 = f32[22,2,128,128]{3,2,1,0:T(8,128)} slice(f32[25,2,128,128]{3,2,1,0:T(8,128)S(1)} %get-tuple-element.44), slice={[0:22], [0:2], [0:128], [0:128]} | slice | bytes 5767168 | tf_op jit(solution)/shard_map/slice | solution.py:260
  123.0 0.0 collective-permute-done
  123.0 0.0 copy-start.10
  123.0 0.6 fusion.1
  123.7 0.0 copy-done.10
  (7 shorter events, 0.1 us)
Async XLA Ops:
  0.6 4.2 %copy-start.5 = (s32[128]{0:T(128)S(1)}, s32[128]{0:T(128)}, u32[]{:S(2)}) copy-start(s32[128]{0:T(128)} %param.15) | copy-start | bytes 1540
  0.6 4.2 %copy-start.4 = (s32[128,1]{0,1:T(1,128)S(1)}, s32[128,1]{0,1:T(1,128)}, u32[]{:S(2)}) copy-start(s32[128,1]{0,1:T(1,128)} %param.14) | copy-start | bytes 1540
  0.7 3.4 %copy-start.8 = (bf16[128,2,4,256]{3,2,1,0:T(4,128)(2,1)S(1)}, bf16[128,2,4,256]{3,2,1,0:T(4,128)(2,1)}, u32[]{:S(2)}) copy-start(bf16[128,2,4,256]{3,2,1,0:T(4,128)(2,1)} %param.11) | copy-start | bytes 1572868
  0.7 3.8 %copy-start.9 = (bf16[128,2,4,256]{3,2,1,0:T(4,128)(2,1)S(1)}, bf16[128,2,4,256]{3,2,1,0:T(4,128)(2,1)}, u32[]{:S(2)}) copy-start(bf16[128,2,4,256]{3,2,1,0:T(4,128)(2,1)} %param.12) | copy-start | bytes 1572868
  0.7 4.2 %copy-start.3 = (bf16[128,256]{1,0:T(8,128)(2,1)S(1)}, bf16[128,256]{1,0:T(8,128)(2,1)}, u32[]{:S(2)}) copy-start(bf16[128,256]{1,0:T(8,128)(2,1)} %refs_3_.1) | copy-start | bytes 196612
  8.5 66.4 %copy-start.2 = (bf16[256,1664]{1,0:T(8,128)(2,1)}, bf16[256,1664]{1,0:T(8,128)(2,1)S(1)}, u32[]{:S(2)}) copy-start(bf16[256,1664]{1,0:T(8,128)(2,1)S(1)} %get-tuple-element.38) | copy-start | bytes 2555908
  75.0 31.4 %all-to-all-start.1 = ((bf16[32,8,1664]{2,1,0:T(8,128)(2,1)}), bf16[32,8,1664]{2,1,0:T(8,128)(2,1)S(1)}, u32[]{:S(2)}, u32[]{:S(2)}) async-start(bf16[32,8,1664]{2,1,0:T(8,128)(2,1)} %bitcast.28), calls=%async_computation.1 | async-start | bytes 1703936 | tf_op jit(solution)/shard_map/all_to_all | solution.py:241
  104.7 1.7 %copy-start.6 = (f32[25,2,128,128]{3,2,1,0:T(8,128)}, f32[25,2,128,128]{3,2,1,0:T(8,128)S(1)}, u32[]{:S(2)}) copy-start(f32[25,2,128,128]{3,2,1,0:T(8,128)S(1)} %get-tuple-element.40.refs_0_) | copy-start | bytes 9830404
  106.4 3.9 %copy-start = (bf16[32,8,1664]{2,1,0:T(8,128)(2,1)}, bf16[32,8,1664]{2,1,0:T(8,128)(2,1)S(1)}, u32[]{:S(2)}) copy-start(bf16[32,8,1664]{2,1,0:T(8,128)(2,1)S(1)} %all-to-all-done.1) | copy-start | bytes 2555908
  106.8 1.9 %copy-start.7 = (f32[25,2,128,128]{3,2,1,0:T(8,128)S(1)}, f32[25,2,128,128]{3,2,1,0:T(8,128)}, u32[]{:S(2)}) copy-start(f32[25,2,128,128]{3,2,1,0:T(8,128)} %copy-done.6) | copy-start | bytes 9830404
  110.3 12.7 %collective-permute-start = (f32[129,128]{1,0:T(8,128)S(1)}, f32[129,128]{1,0:T(8,128)S(1)}, u32[]{:S(2)}, u32[]{:S(2)}) collective-permute-start(f32[129,128]{1,0:T(8,128)S(1)} %pad_maximum_fusion), channel_id=1, source_target_pairs={{0,1},{1,2},{2,3},{3,4},{4,5},{5,6},{6,7},{7,8},{8,9},{9,10},{10,1... | collective-permute-start | bytes 198152 | tf_op jit(solution)/shard_map/ppermute | solution.py:258
  110.6 1.2 copy-start.1
  123.0 0.7 copy-start.10

commit v5 on v4

--- a/solution.py
+++ b/solution.py
@@ -143,7 +143,7 @@
             pltpu.SMEM((slots + 8,), jnp.int32),
             pltpu.SMEM((slots + 8,), jnp.int32),
         ],
-        compiler_params=pltpu.CompilerParams(vmem_limit_bytes=40 * 1024 * 1024),
+        compiler_params=pltpu.CompilerParams(vmem_limit_bytes=20 * 1024 * 1024),
         cost_estimate=pl.CostEstimate(
             flops=slots * 20 * 1000 * 1000 * width // 256, bytes_accessed=10 * 1000 * 1000, transcendentals=0
         ),
@@ -151,11 +151,15 @@
 
 
 def send_kernel(parts, waves, *refs):
-    index_ref, frac_ref, proj_ref, force_ref, owner_col, offset_col, owner_row, offset_row = refs[:8]
-    out_refs, payload_ref = refs[8:-1], refs[-1]
+    index_ref, frac_ref, proj_ref, force_ref, owner_row, offset_row = refs[:6]
+    out_refs, payload_ref = refs[6:-1], refs[-1]
     slot_width, neighbors, lanes = parts
     pieces = slot_width * lanes
     count = index_ref.shape[0]
+    shape = (count, count)
+    owner_col = jnp.broadcast_to(owner_row[...].astype(jnp.float32), shape).T
+    offset_col = jnp.broadcast_to(offset_row[...].astype(jnp.float32), shape).T
+    tag = (offset_col[:, :128] + 1.0).astype(jnp.bfloat16)
     for s in range(slot_width):
         for lane in range(lanes):
             piece = s * lanes + lane
@@ -169,15 +173,13 @@
             if s == 0:
                 payload_ref[at, column : column + 128] = force_ref[:, lane * 128 : lane * 128 + 128]
             else:
-                tag = jnp.broadcast_to((offset_col[...] + 1).astype(jnp.float32), (count, 128))
-                payload_ref[at, column : column + 128] = tag.astype(jnp.bfloat16)
-
-    shape = (count, count)
+                payload_ref[at, column : column + 128] = tag
+
     other_at = lax.broadcasted_iota(jnp.int32, shape, 0)
     row_at = lax.broadcasted_iota(jnp.int32, shape, 1)
-    other_key = jnp.where(offset_col[...] == BLK_DEV - 1, 0, count) + other_at
+    other_key = jnp.where(offset_col == BLK_DEV - 1, 0, count) + other_at
     row_key = jnp.where(offset_row[...] == BLK_DEV - 1, 0, count) + row_at
-    before = (owner_col[...] == owner_row[...]) & (other_key < row_key)
+    before = (owner_col == owner_row[...].astype(jnp.float32)) & (other_key < row_key)
     position = jnp.sum(jnp.where(before, 1.0, 0.0), axis=0, keepdims=True).astype(jnp.int32)
 
     first = 0
@@ -197,7 +199,7 @@
         first += size
 
 
-def send_blocks(index, frac, proj, forces, owner_col, offset_col, owner_row, offset_row, parts, waves, device_count):
+def send_blocks(index, frac, proj, forces, owner_row, offset_row, parts, waves, device_count):
     slot_width, neighbors, lanes = parts
     pieces = slot_width * lanes
     width = (3 * neighbors + 1) * 128
@@ -205,11 +207,11 @@
     return pl.pallas_call(
         functools.partial(send_kernel, parts, waves),
         out_shape=[jax.ShapeDtypeStruct((device_count * size * pieces, width), jnp.bfloat16) for size in waves],
-        in_specs=[vmem] * 8,
+        in_specs=[vmem] * 6,
         out_specs=[vmem] * len(waves),
         scratch_shapes=[pltpu.VMEM((pieces * index.shape[0], width), jnp.bfloat16)],
-        compiler_params=pltpu.CompilerParams(vmem_limit_bytes=40 * 1024 * 1024),
-    )(index, frac, proj, forces, owner_col, offset_col, owner_row, offset_row)
+        compiler_params=pltpu.CompilerParams(vmem_limit_bytes=20 * 1024 * 1024),
+    )(index, frac, proj, forces, owner_row, offset_row)
 
 
 def on_device(spline_index, spline_frac, projection, forces, row_owner, row_offset):
@@ -228,8 +230,6 @@
         spline_frac.reshape(flat),
         projection.reshape(flat),
         forces,
-        row_owner,
-        row_offset[:, None],
         row_owner.reshape(1, row_count),
         row_offset[None, :],
         (slot_width, neighbors, lanes),

time: 125 us -> 124 us (level)
  local copies, waits for them, and re-layouts: 9.88 us -> 8.26 us
    unnamed x24 -> x23, local copies, waits for them, and re-layouts: 5.55 us -> 4.79 us
where the time goes in v5:
time: 124 us; the launch traced here: 122 us
  blocking collectives  66.4 us (54%)
  Pallas kernels  40.9 us (33%)
  local copies, waits for them, and re-layouts  8.26 us (7%)
  starting transfers between devices  3.22 us (3%)
  other arithmetic  2.51 us (2%)
    all_to_all x1, blocking collectives, exchange(): return lax.all_to_all(block, AXES, split_axis=0, concat_axis=0, tiled=True)  66.4 us
    pallas_call x3, Pallas kernels, normal_sums(): pl.pallas_call(functools.partial(normal_kernel, neighbors, width, pick),...  37.2 us
    unnamed x23, local copies, waits for them, and re-layouts  4.79 us
    pallas_call x1, Pallas kernels, send_blocks(): pl.pallas_call(functools.partial(send_kernel, parts, waves), out_shape=[j...  3.61 us
    all_to_all x1, starting transfers between devices, exchange(): return lax.all_to_all(block, AXES, split_axis=0, concat_axis=0, tiled=True)  2.9 us
  transfers between devices with their start and end apart: 2, of which 0 were waited for; matrix products, arithmetic and copies ran while one was open for 2% of the time, Pallas kernels for 29%

profile of v5, /device:TPU:0, one launch (start us, length us, event | category | flops | bytes accessed | tf_op | source)
XLA Modules:
  0.0 122.1 jit_solution(11225332176983163925)
XLA Ops:
  0.6 0.0 copy-start.8
  0.6 0.0 copy-start.9
  0.7 0.0 copy-start.5
  0.7 0.0 copy-start.4
  0.7 0.0 copy-start.3
  0.7 1.5 %convert_element_type.14 = bf16[128,2,4,256]{3,2,1,0:T(4,128)(2,1)S(1)} convert(s32[128,2,4,256]{3,2,1,0:T(4,128)} %param.10) | non-fusion elementwise | flops 262144 | bytes 1572864 | tf_op jit(solution)/shard_map/convert_element_type | solution.py:229
  2.2 0.4 reshape.90.refs_0_
  2.6 0.0 copy-done.8
  2.6 0.4 reshape.91.refs_1_
  3.0 0.0 copy-done.9
  3.0 0.4 reshape.92.refs_2_
  3.3 0.0 copy-done.5
  3.4 0.0 copy-done.4
  3.4 0.0 copy-done.3
  3.4 3.6 %shard_map.77 = (bf16[768,1664]{1,0:T(8,128)(2,1)S(1)}, bf16[256,1664]{1,0:T(8,128)(2,1)S(1)}) custom-call(bf16[128,2048]{1,0:T(8,128)(2,1)S(1)} %reshape.90.refs_0_, bf16[128,2048]{1,0:T(8,128)(2,1)S(1)} %reshape.91.refs_1_, bf16[128,2048]{1,0:T(8,128)(2,1)S(1)} %reshape.92.refs_2_, bf16[128,256]{1,0:T(8,128)(2,1)S(1)} %copy-done.3, s32[1,128]{1,0:T(1,128)S(1)} %bitcast.28, ...), custom_call_target="tpu_custom_call" | custom-call | tf_op jit(solution)/shard_map/pallas_call | solution.py:207
  7.0 0.0 copy-start.2
  7.0 66.4 %all_to_all.23 = bf16[32,24,1664]{2,1,0:T(8,128)(2,1)S(1)} all-to-all(bf16[32,24,1664]{2,1,0:T(8,128)(2,1)S(1)} %bitcast.23), channel_id=1, replica_groups=mesh['frame'=4,'panel'=8] {'frame','panel'}, dimensions={0} | all-to-all | bytes 5111808 | tf_op jit(solution)/shard_map/all_to_all | solution.py:241
  73.4 0.0 copy-done.2
  73.4 2.9 %all-to-all-start.1 = ((bf16[32,8,1664]{2,1,0:T(8,128)(2,1)}), bf16[32,8,1664]{2,1,0:T(8,128)(2,1)S(1)}, u32[]{:S(2)}, u32[]{:S(2)}) async-start(bf16[32,8,1664]{2,1,0:T(8,128)(2,1)} %bitcast.27), calls=%async_computation.1 | async-start | bytes 1703936 | tf_op jit(solution)/shard_map/all_to_all | solution.py:241
  76.3 0.1 slice_reduce_fusion
  76.5 0.1 reshape_squeeze.8
  76.6 0.2 convert_reduce_fusion.where_ref
  76.8 26.4 %shard_map.78 = (f32[25,2,128,128]{3,2,1,0:T(8,128)S(1)}, f32[25,8,128]{2,1,0:T(8,128)S(1)}) custom-call(s32[192]{0:T(256)S(1)} %convert_reduce_fusion.where_ref, bf16[768,1664]{1,0:T(8,128)(2,1)S(1)} %bitcast.22), custom_call_target="tpu_custom_call" | custom-call | flops 3840000000 | bytes 10000000 | tf_op jit(solution)/shard_map/pallas_call | solution.py:129
  103.2 0.0 copy-start.6
  103.2 1.7 %copy-done.6 = f32[25,2,128,128]{3,2,1,0:T(8,128)} copy-done((f32[25,2,128,128]{3,2,1,0:T(8,128)}, f32[25,2,128,128]{3,2,1,0:T(8,128)S(1)}, u32[]{:S(2)}) %copy-start.6) | copy-done | bytes 3276824
  104.8 0.0 all-to-all-done.1
  104.8 0.0 copy-start
  104.9 0.1 slice_reduce_fusion.1
  105.0 0.1 reshape_squeeze.7
  105.1 0.2 convert_reduce_fusion.1.where_ref
  105.3 0.0 copy-start.7
  105.3 1.9 %copy-done.7 = f32[25,2,128,128]{3,2,1,0:T(8,128)S(1)} copy-done((f32[25,2,128,128]{3,2,1,0:T(8,128)S(1)}, f32[25,2,128,128]{3,2,1,0:T(8,128)}, u32[]{:S(2)}) %copy-start.7) | copy-done | bytes 3276824
  107.2 1.5 %shard_map.79 = (f32[25,2,128,128]{3,2,1,0:T(8,128)S(1)}, f32[25,8,128]{2,1,0:T(8,128)S(1)}) custom-call(s32[64]{0:T(128)S(1)} %convert_reduce_fusion.1.where_ref, bf16[256,1664]{1,0:T(8,128)(2,1)S(1)} %bitcast.25, f32[25,2,128,128]{3,2,1,0:T(8,128)S(1)} %copy-done.7, f32[25,8,128]{2,1,0:T(8,128)S(1)} %get-tuple-element.41.refs_1_), custom_call_target="tpu_custom_call" | custom-call | flops 1280000000 | bytes 10000000 | tf_op jit(solution)/shard_map/pallas_call | solution.py:129
  108.7 0.0 copy-done
  108.7 0.3 collective-permute-start
  109.0 0.0 copy-start.1
  109.1 1.2 copy-done.1
  110.2 9.4 %shard_map.80 = (f32[25,2,128,128]{3,2,1,0:T(8,128)S(1)}, f32[25,8,128]{2,1,0:T(8,128)S(1)}) custom-call(s32[64]{0:T(128)S(1)} %convert_reduce_fusion.1.where_ref, bf16[256,1664]{1,0:T(8,128)(2,1)S(1)} %bitcast.26, f32[25,2,128,128]{3,2,1,0:T(8,128)S(1)} %get-tuple-element.42.refs_0_, f32[25,8,128]{2,1,0:T(8,128)S(1)} %get-tuple-element.43.refs_1_), custom_call_target="tpu_custom_call" | custom-call | flops 1280000000 | bytes 10000000 | tf_op jit(solution)/shard_map/pallas_call | solution.py:129
  119.7 1.8 %slice.84 = f32[22,2,128,128]{3,2,1,0:T(8,128)} slice(f32[25,2,128,128]{3,2,1,0:T(8,128)S(1)} %get-tuple-element.44), slice={[0:22], [0:2], [0:128], [0:128]} | slice | bytes 5767168 | tf_op jit(solution)/shard_map/slice | solution.py:260
  121.4 0.0 collective-permute-done
  121.5 0.0 copy-start.10
  121.5 0.6 fusion.1
  122.1 0.0 copy-done.10
  (7 shorter events, 0.1 us)
Async XLA Ops:
  0.6 1.9 %copy-start.8 = (bf16[128,2,4,256]{3,2,1,0:T(4,128)(2,1)S(1)}, bf16[128,2,4,256]{3,2,1,0:T(4,128)(2,1)}, u32[]{:S(2)}) copy-start(bf16[128,2,4,256]{3,2,1,0:T(4,128)(2,1)} %param.11) | copy-start | bytes 1572868
  0.6 2.3 %copy-start.9 = (bf16[128,2,4,256]{3,2,1,0:T(4,128)(2,1)S(1)}, bf16[128,2,4,256]{3,2,1,0:T(4,128)(2,1)}, u32[]{:S(2)}) copy-start(bf16[128,2,4,256]{3,2,1,0:T(4,128)(2,1)} %param.12) | copy-start | bytes 1572868
  0.7 2.7 %copy-start.5 = (s32[128]{0:T(128)S(1)}, s32[128]{0:T(128)}, u32[]{:S(2)}) copy-start(s32[128]{0:T(128)} %param.15) | copy-start | bytes 1540
  0.7 2.7 %copy-start.4 = (s32[128,1]{0,1:T(1,128)S(1)}, s32[128,1]{0,1:T(1,128)}, u32[]{:S(2)}) copy-start(s32[128,1]{0,1:T(1,128)} %param.14) | copy-start | bytes 1540
  0.7 2.7 %copy-start.3 = (bf16[128,256]{1,0:T(8,128)(2,1)S(1)}, bf16[128,256]{1,0:T(8,128)(2,1)}, u32[]{:S(2)}) copy-start(bf16[128,256]{1,0:T(8,128)(2,1)} %refs_3_.1) | copy-start | bytes 196612
  7.0 66.4 %copy-start.2 = (bf16[256,1664]{1,0:T(8,128)(2,1)}, bf16[256,1664]{1,0:T(8,128)(2,1)S(1)}, u32[]{:S(2)}) copy-start(bf16[256,1664]{1,0:T(8,128)(2,1)S(1)} %get-tuple-element.38) | copy-start | bytes 2555908
  73.4 31.4 %all-to-all-start.1 = ((bf16[32,8,1664]{2,1,0:T(8,128)(2,1)}), bf16[32,8,1664]{2,1,0:T(8,128)(2,1)S(1)}, u32[]{:S(2)}, u32[]{:S(2)}) async-start(bf16[32,8,1664]{2,1,0:T(8,128)(2,1)} %bitcast.27), calls=%async_computation.1 | async-start | bytes 1703936 | tf_op jit(solution)/shard_map/all_to_all | solution.py:241
  103.2 1.7 %copy-start.6 = (f32[25,2,128,128]{3,2,1,0:T(8,128)}, f32[25,2,128,128]{3,2,1,0:T(8,128)S(1)}, u32[]{:S(2)}) copy-start(f32[25,2,128,128]{3,2,1,0:T(8,128)S(1)} %get-tuple-element.40.refs_0_) | copy-start | bytes 9830404
  104.8 3.9 %copy-start = (bf16[32,8,1664]{2,1,0:T(8,128)(2,1)}, bf16[32,8,1664]{2,1,0:T(8,128)(2,1)S(1)}, u32[]{:S(2)}) copy-start(bf16[32,8,1664]{2,1,0:T(8,128)(2,1)S(1)} %all-to-all-done.1) | copy-start | bytes 2555908
  105.3 1.9 %copy-start.7 = (f32[25,2,128,128]{3,2,1,0:T(8,128)S(1)}, f32[25,2,128,128]{3,2,1,0:T(8,128)}, u32[]{:S(2)}) copy-start(f32[25,2,128,128]{3,2,1,0:T(8,128)} %copy-done.6) | copy-start | bytes 9830404
  108.7 12.7 %collective-permute-start = (f32[129,128]{1,0:T(8,128)S(1)}, f32[129,128]{1,0:T(8,128)S(1)}, u32[]{:S(2)}, u32[]{:S(2)}) collective-permute-start(f32[129,128]{1,0:T(8,128)S(1)} %pad_maximum_fusion), channel_id=1, source_target_pairs={{0,1},{1,2},{2,3},{3,4},{4,5},{5,6},{6,7},{7,8},{8,9},{9,10},{10,1... | collective-permute-start | bytes 198152 | tf_op jit(solution)/shard_map/ppermute | solution.py:258
  109.0 1.2 copy-start.1
  121.5 0.7 copy-start.10
